TPU v7x, 32 devices: a whole 2x2x4 slice. The times are simulated.
32 devices in a mesh: beam: 2 (over y), bin: 4 (over z), chan: 4 (over x, core).
Axes of the slice: x: 2, y: 2, z: 4, core: 2. Of those that a mesh axis runs over, the one named last changes fastest.
Arguments:
- spectra: bfloat16 [2, 8192, 1024], P(None, ('beam', 'chan', 'bin')), parts along dimension 1, may hold values from -6 to 6
- dm_trials: int32 [64], replicated, may hold values from 0 to 1023
- chan_delay: int32 [4096], replicated, may hold values from 0 to 32767
- template_bank: bfloat16 [2, 256, 256], replicated, may hold values from -0.25 to 0.25
- template_ids: int32 [128], replicated, may hold values from 0 to 255
Outputs:
- powers: bfloat16 [128, 128, 1024], P(('beam', 'chan'), None, 'bin'), parts along dimension 0
There are 2 independent parts, one for each index of `beam`. A program takes and returns all parts, laid end to end along the dimension named above; an argument that names none is the same for every part. Nothing has to cross between parts.
All inputs are finite; a program needn't handle non-finite values.
Results may differ from a plain program's by a relative error of at most 0.0095.
Values may be sent and summed in bfloat16 or wider, within the bound.
No kernel may reach another device: no remote copies, remote signals or barrier semaphores. Data moves between devices by JAX's collectives and lax.ppermute only.
A program may use at most 64 MiB of HBM per device.

v0:
```python
import math

import jax
import jax.numpy as jnp
from jax import lax
from jax.sharding import PartitionSpec as P

EDGE = 128


def with_halo(cells, sides, width):
    for axis, dim in sides:
        count = lax.axis_size(axis)
        ends = count - 1
        head = lax.slice_in_dim(cells, 0, width, axis=dim)
        tail = lax.slice_in_dim(cells, cells.shape[dim] - width, cells.shape[dim], axis=dim)
        cells = jnp.concatenate(
            [
                lax.ppermute(tail, axis, [(i, (i + 1) % count) for i in range(ends)]),
                cells,
                lax.ppermute(head, axis, [((i + 1) % count, i) for i in range(ends)]),
            ],
            axis=dim,
        )
    return cells


def dedisperse(spec_local, delays, first_bin, samples):
    bin_count = spec_local.shape[2]
    block_size = math.gcd(bin_count, 32)
    trial_count = delays.shape[0]

    def one_block(block_index):
        offset = block_index * block_size
        spec_part = lax.dynamic_slice_in_dim(spec_local, offset, block_size, 2)
        bin_ids = first_bin + offset + jnp.arange(block_size, dtype=jnp.int32)
        turn_counts = bin_ids[:, None, None] * delays[None, :, :] % samples
        angles = turn_counts.astype(jnp.float32) * (2.0 * math.pi / samples)
        cosine = jnp.cos(angles).astype(jnp.bfloat16)
        sine_part = (-jnp.sin(angles)).astype(jnp.bfloat16)
        real_part = jnp.einsum(
            "fdc,cf->df", cosine, spec_part[0], preferred_element_type=jnp.float32
        ) - jnp.einsum("fdc,cf->df", sine_part, spec_part[1], preferred_element_type=jnp.float32)
        imag_part = jnp.einsum(
            "fdc,cf->df", cosine, spec_part[1], preferred_element_type=jnp.float32
        ) + jnp.einsum("fdc,cf->df", sine_part, spec_part[0], preferred_element_type=jnp.float32)
        return jnp.stack([real_part, imag_part], 1)

    pieces = lax.map(one_block, jnp.arange(bin_count // block_size, dtype=jnp.int32))
    return pieces.transpose(1, 2, 0, 3).reshape(trial_count, 2, bin_count)


def template_kernel(template_bank, template_ids):
    bank_size = template_bank.shape[1]
    one_hot = (template_ids[:, None] == jnp.arange(bank_size, dtype=jnp.int32)[None, :]).astype(
        jnp.bfloat16
    )
    chosen_re = jnp.dot(one_hot, template_bank[0], preferred_element_type=jnp.float32).astype(
        jnp.bfloat16
    )
    chosen_im = jnp.dot(one_hot, template_bank[1], preferred_element_type=jnp.float32).astype(
        jnp.bfloat16
    )
    upper = jnp.stack([chosen_re, -chosen_im], 1)
    lower = jnp.stack([chosen_im, chosen_re], 1)
    return jnp.concatenate([upper, lower], 0)


def correlate(signal, kernel):
    return lax.conv_general_dilated(
        signal,
        kernel,
        (1,),
        "VALID",
        dimension_numbers=("NCH", "OIH", "NCH"),
        preferred_element_type=jnp.float32,
    )


def local(spectra, dm_trials, chan_delay, template_bank, template_ids):
    samples = 2 * spectra.shape[2]
    bin_count = spectra.shape[2] // lax.axis_size("bin")
    scale = 1.0 / math.sqrt(chan_delay.shape[0])
    gathered = lax.all_to_all(spectra, "bin", split_axis=2, concat_axis=1, tiled=True)
    chan_count = gathered.shape[1]
    own_delay = lax.dynamic_slice_in_dim(
        chan_delay, lax.axis_index("chan") * chan_count, chan_count
    )
    first_bin = lax.axis_index("bin") * bin_count
    delays = dm_trials[:, None] * own_delay[None, :] % samples
    summed = lax.psum_scatter(
        dedisperse(gathered, delays, first_bin, samples), "chan", scatter_dimension=0, tiled=True
    )
    dedispersed = (summed * scale).astype(jnp.bfloat16)
    kernel = template_kernel(template_bank, template_ids)
    reach = kernel.shape[2] // 2
    padded = with_halo(dedispersed, (("bin", 2),), EDGE)
    response = correlate(padded[:, :, : bin_count + 2 * reach - 1], kernel)
    half_rows = kernel.shape[0] // 2
    real_resp = response[:, :half_rows]
    imag_resp = response[:, half_rows:]
    return (real_resp * real_resp + imag_resp * imag_resp).astype(jnp.bfloat16)


def solution(mesh):
    in_specs = (P(None, ("beam", "chan", "bin"), None), P(), P(), P(), P())
    out_specs = P(("beam", "chan"), None, "bin")
    return jax.shard_map(local, mesh=mesh, in_specs=in_specs, out_specs=out_specs, check_vma=False)
```

profile of v0, /device:TPU:0, one launch (start us, length us, event | category | flops | bytes accessed | tf_op | source)
XLA Modules:
  0.0 448.7 jit_solution(1031698361331119498)
XLA Ops:
  6.5 3.7 copy.37
  10.2 6.3 %all-to-all-start = ((bf16[2,256,1024]{1,0,2:T(2,128)(2,1)}), bf16[2,256,1024]{1,0,2:T(2,128)(2,1)S(1)}, u32[]{:S(2)}, u32[]{:S(2)}) async-start(bf16[2,256,1024]{1,0,2:T(2,128)(2,1)} %copy.37), calls=%async_computation | async-start | bytes 2097152 | tf_op jit(solution)/shard_map/all_to_all | solution.py:84
  16.6 0.6 dynamic-slice
  17.9 0.7 dynamic_slice.16
  18.6 0.2 convolution_convert_fusion
  18.8 23.5 %all-to-all-done = bf16[2,256,1024]{1,0,2:T(2,128)(2,1)S(1)} async-done(((bf16[2,256,1024]{1,0,2:T(2,128)(2,1)}), bf16[2,256,1024]{1,0,2:T(2,128)(2,1)S(1)}, u32[]{:S(2)}, u32[]{:S(2)}) %all-to-all-start) | async-done | bytes 1048608 | tf_op jit(solution)/shard_map/all_to_all | solution.py:84
  42.3 0.7 copy.38
  43.1 343.3 %while.13 = (s32[]{:T(128)}, f32[8,64,2,32]{3,2,1,0:T(2,128)S(1)}, s32[8]{0:T(128)S(1)}, bf16[2,1024,256]{2,1,0:T(8,128)(2,1)S(1)}, s32[]{:T(128)}, /*index=5*/s...) while((s32[]{:T(128)}, f32[8,64,2,32]{3,2,1,0:T(2,128)S(1)}, ...), condition=%wide.region_1.2_spmd.clone, body=%wide.region_0.1_spmd.clone.sunk | while | flops 57475112 | bytes 1987295 | solution.py:49
  43.1 0.6 dynamic_slice.20
  44.3 0.2 add_select_fusion.3
  44.5 0.2 fusion.32
  44.7 0.2 copy.80
  44.9 0.2 copy.81
  45.1 40.4 %fusion.33 = (f32[32,64]{1,0:T(8,128)S(1)}, f32[32,64]{1,0:T(8,128)S(1)}, f32[32,64]{1,0:T(8,128)S(1)}, f32[32,64]{1,0:T(8,128)S(1)}) fusion(f32[32,1024]{1,0:T(8,128)S(1)} %copy.80, s32[64,1024]{1,0:T(8,128)S(1)} %add_select_fusion.3, s32[32]{0:T(128)S(1)} %iota_add_fusion.2, f32[32,1024]{1,0:T(8,128)S(1)} %copy.81), kind=kLoop, calls=%fused_computation.12.clone.1 | loop fusion | flops 56614912 | bytes 557184 | tf_op jit(solution)/shard_map/while
  86.0 0.6 dynamic_slice.20
  87.2 0.2 add_select_fusion.3
  87.4 0.2 fusion.32
  87.6 0.2 copy.80
  87.8 0.2 copy.81
  88.0 40.4 %fusion.33 = (f32[32,64]{1,0:T(8,128)S(1)}, f32[32,64]{1,0:T(8,128)S(1)}, f32[32,64]{1,0:T(8,128)S(1)}, f32[32,64]{1,0:T(8,128)S(1)}) fusion(f32[32,1024]{1,0:T(8,128)S(1)} %copy.80, s32[64,1024]{1,0:T(8,128)S(1)} %add_select_fusion.3, s32[32]{0:T(128)S(1)} %iota_add_fusion.2, f32[32,1024]{1,0:T(8,128)S(1)} %copy.81), kind=kLoop, calls=%fused_computation.12.clone.1 | loop fusion | flops 56614912 | bytes 557184 | tf_op jit(solution)/shard_map/while
  128.9 0.6 dynamic_slice.20
  130.2 0.2 add_select_fusion.3
  130.3 0.2 fusion.32
  130.6 0.2 copy.80
  130.7 0.2 copy.81
  130.9 40.4 %fusion.33 = (f32[32,64]{1,0:T(8,128)S(1)}, f32[32,64]{1,0:T(8,128)S(1)}, f32[32,64]{1,0:T(8,128)S(1)}, f32[32,64]{1,0:T(8,128)S(1)}) fusion(f32[32,1024]{1,0:T(8,128)S(1)} %copy.80, s32[64,1024]{1,0:T(8,128)S(1)} %add_select_fusion.3, s32[32]{0:T(128)S(1)} %iota_add_fusion.2, f32[32,1024]{1,0:T(8,128)S(1)} %copy.81), kind=kLoop, calls=%fused_computation.12.clone.1 | loop fusion | flops 56614912 | bytes 557184 | tf_op jit(solution)/shard_map/while
  171.8 0.6 dynamic_slice.20
  173.1 0.2 add_select_fusion.3
  173.3 0.2 fusion.32
  173.5 0.2 copy.80
  173.6 0.2 copy.81
  173.8 40.4 %fusion.33 = (f32[32,64]{1,0:T(8,128)S(1)}, f32[32,64]{1,0:T(8,128)S(1)}, f32[32,64]{1,0:T(8,128)S(1)}, f32[32,64]{1,0:T(8,128)S(1)}) fusion(f32[32,1024]{1,0:T(8,128)S(1)} %copy.80, s32[64,1024]{1,0:T(8,128)S(1)} %add_select_fusion.3, s32[32]{0:T(128)S(1)} %iota_add_fusion.2, f32[32,1024]{1,0:T(8,128)S(1)} %copy.81), kind=kLoop, calls=%fused_computation.12.clone.1 | loop fusion | flops 56614912 | bytes 557184 | tf_op jit(solution)/shard_map/while
  214.7 0.6 dynamic_slice.20
  216.0 0.2 add_select_fusion.3
  216.2 0.2 fusion.32
  216.6 0.2 copy.81
  216.7 40.4 %fusion.33 = (f32[32,64]{1,0:T(8,128)S(1)}, f32[32,64]{1,0:T(8,128)S(1)}, f32[32,64]{1,0:T(8,128)S(1)}, f32[32,64]{1,0:T(8,128)S(1)}) fusion(f32[32,1024]{1,0:T(8,128)S(1)} %copy.80, s32[64,1024]{1,0:T(8,128)S(1)} %add_select_fusion.3, s32[32]{0:T(128)S(1)} %iota_add_fusion.2, f32[32,1024]{1,0:T(8,128)S(1)} %copy.81), kind=kLoop, calls=%fused_computation.12.clone.1 | loop fusion | flops 56614912 | bytes 557184 | tf_op jit(solution)/shard_map/while
  257.7 0.6 dynamic_slice.20
  258.9 0.2 add_select_fusion.3
  259.1 0.2 fusion.32
  259.5 0.2 copy.81
  259.7 40.4 %fusion.33 = (f32[32,64]{1,0:T(8,128)S(1)}, f32[32,64]{1,0:T(8,128)S(1)}, f32[32,64]{1,0:T(8,128)S(1)}, f32[32,64]{1,0:T(8,128)S(1)}) fusion(f32[32,1024]{1,0:T(8,128)S(1)} %copy.80, s32[64,1024]{1,0:T(8,128)S(1)} %add_select_fusion.3, s32[32]{0:T(128)S(1)} %iota_add_fusion.2, f32[32,1024]{1,0:T(8,128)S(1)} %copy.81), kind=kLoop, calls=%fused_computation.12.clone.1 | loop fusion | flops 56614912 | bytes 557184 | tf_op jit(solution)/shard_map/while
  300.6 0.6 dynamic_slice.20
  301.8 0.2 add_select_fusion.3
  302.0 0.2 fusion.32
  302.4 0.2 copy.81
  302.6 40.4 %fusion.33 = (f32[32,64]{1,0:T(8,128)S(1)}, f32[32,64]{1,0:T(8,128)S(1)}, f32[32,64]{1,0:T(8,128)S(1)}, f32[32,64]{1,0:T(8,128)S(1)}) fusion(f32[32,1024]{1,0:T(8,128)S(1)} %copy.80, s32[64,1024]{1,0:T(8,128)S(1)} %add_select_fusion.3, s32[32]{0:T(128)S(1)} %iota_add_fusion.2, f32[32,1024]{1,0:T(8,128)S(1)} %copy.81), kind=kLoop, calls=%fused_computation.12.clone.1 | loop fusion | flops 56614912 | bytes 557184 | tf_op jit(solution)/shard_map/while
  343.5 0.6 dynamic_slice.20
  344.7 0.2 add_select_fusion.3
  344.9 0.2 fusion.32
  345.3 0.2 copy.81
  345.5 40.4 %fusion.33 = (f32[32,64]{1,0:T(8,128)S(1)}, f32[32,64]{1,0:T(8,128)S(1)}, f32[32,64]{1,0:T(8,128)S(1)}, f32[32,64]{1,0:T(8,128)S(1)}) fusion(f32[32,1024]{1,0:T(8,128)S(1)} %copy.80, s32[64,1024]{1,0:T(8,128)S(1)} %add_select_fusion.3, s32[32]{0:T(128)S(1)} %iota_add_fusion.2, f32[32,1024]{1,0:T(8,128)S(1)} %copy.81), kind=kLoop, calls=%fused_computation.12.clone.1 | loop fusion | flops 56614912 | bytes 557184 | tf_op jit(solution)/shard_map/while
  386.4 0.2 copy.39
  386.6 0.8 copy.40
  387.4 0.2 fusion.17
  387.6 30.5 %all-reduce.3.cloned.1.call-done = f32[64,2,256]{2,1,0:T(2,128)} async-done(((f32[64,2,256]{2,1,0:T(2,128)}), f32[64,2,256]{2,1,0:T(2,128)}) %all-reduce.3.cloned.1.call-update) | async-done | bytes 131088
  418.1 0.8 constant_dynamic-slice_fusion
  418.8 3.4 collective-permute-start
  422.2 1.5 collective-permute-start.1
  423.7 0.2 copy.43
  423.9 3.8 collective-permute-done.1
  428.0 12.0 %fusion.26 = f32[16,256,256]{1,0,2:T(8,128)S(1)} fusion(bf16[16,2,512]{0,1,2:T(2,128)(2,1)S(1)} %copy.42, bf16[256,2,256]{0,1,2:T(2,128)(2,1)S(1)} %copy.43), kind=kOutput, calls=%fused_computation.55 | convolution fusion | flops 1073741824 | bytes 4489216 | tf_op jit(solution)/shard_map/conv_general_dilated | solution.py:70
  440.0 0.3 fusion.16
  440.2 1.6 copy.44
  (87 shorter events, 4.5 us)
Async XLA Ops:
  6.5 10.0 %copy-start.3 = (u32[32]{0:T(128)S(1)}, u32[32]{0:T(128)}, u32[]{:S(2)}) copy-start(u32[32]{0:T(128)} %constant.90) | copy-start | bytes 388
  6.5 12.0 %copy-start.2 = (s32[128]{0:T(128)S(1)}, s32[128]{0:T(128)}, u32[]{:S(2)}) copy-start(s32[128]{0:T(128)} %param.11) | copy-start | bytes 1540
  6.5 12.0 %copy-start.1 = (bf16[2,256,256]{2,1,0:T(8,128)(2,1)S(1)}, bf16[2,256,256]{2,1,0:T(8,128)(2,1)}, u32[]{:S(2)}) copy-start(bf16[2,256,256]{2,1,0:T(8,128)(2,1)} %param.10) | copy-start | bytes 786436
  6.5 36.5 %copy-start = (s32[64]{0:T(128)S(1)}, s32[64]{0:T(128)}, u32[]{:S(2)}) copy-start(s32[64]{0:T(128)} %param.8) | copy-start | bytes 772
  10.2 32.0 %all-to-all-start = ((bf16[2,256,1024]{1,0,2:T(2,128)(2,1)}), bf16[2,256,1024]{1,0,2:T(2,128)(2,1)S(1)}, u32[]{:S(2)}, u32[]{:S(2)}) async-start(bf16[2,256,1024]{1,0,2:T(2,128)(2,1)} %copy.37), calls=%async_computation | async-start | bytes 2097152 | tf_op jit(solution)/shard_map/all_to_all | solution.py:84
  16.6 401.5 %all-reduce.3.cloned.1.call-start = ((), (), s32[]{:S(2)}) async-start(), calls=%async_computation.1 | async-start | bytes 262144
  418.8 5.1 %collective-permute-start = (bf16[16,2,128]{2,0,1:T(8,128)(2,1)S(1)}, bf16[16,2,128]{2,0,1:T(8,128)(2,1)S(1)}, u32[]{:S(2)}, u32[]{:S(2)}) collective-permute-start(bf16[16,2,128]{2,0,1:T(8,128)(2,1)S(1)} %get-tuple-element.124), channel_id=1, source_target_pairs={{0,4},{4,8},{8,12},{1,5},{5,9},{9,13},{2,6},{6,10},{10,14},{3,7},{... | collective-permute-start | bytes 24584 | tf_op jit(solution)/shard_map/ppermute | solution.py:19
  422.2 5.5 %collective-permute-start.1 = (bf16[16,2,128]{2,0,1:T(8,128)(2,1)S(1)}, bf16[16,2,128]{2,0,1:T(8,128)(2,1)S(1)}, u32[]{:S(2)}, u32[]{:S(2)}) collective-permute-start(bf16[16,2,128]{2,0,1:T(8,128)(2,1)S(1)} %get-tuple-element.125), channel_id=1, source_target_pairs={{4,0},{8,4},{12,8},{5,1},{9,5},{13,9},{6,2},{10,6},{14,10},{7,3},{... | collective-permute-start | bytes 24584 | tf_op jit(solution)/shard_map/ppermute | solution.py:21
Sparse Core Ops, SparseCore 0:
  387.5 30.4 all-reduce.2
where the time goes:
time: 449 us
  other arithmetic  328 us (73%)
  waiting for transfers between devices  57.8 us (13%)
  local copies, waits for them, and re-layouts  19.5 us (4%)
  between operations  14.1 us (3%)
  matrix products  12.4 us (3%)
  starting transfers between devices  11.2 us (2%)
  loops' own time  5.74 us (1%)
    while x16, other arithmetic  325 us
    unnamed x2, waiting for transfers between devices  30.5 us
    all_to_all x1, waiting for transfers between devices, local(): lax.all_to_all(spectra, 'bin', split_axis=2, concat_axis=1, tiled=True)  23.5 us
    conv_general_dilated x1, matrix products, correlate(): lax.conv_general_dilated(signal, kernel, (1,), 'VALID', dimension_numbers...  12 us
  transfers between devices with their start and end apart: 4, of which 3 were waited for; matrix products, arithmetic and copies ran while one was open for 0% of the time, Pallas kernels for 0%

commit v1 on v0

v1 whole, which is shorter than its diff:
```python
import functools
import math

import jax
import jax.numpy as jnp
from jax import lax
from jax.experimental import pallas as pl
from jax.experimental.pallas import tpu as pltpu
from jax.sharding import PartitionSpec as P

EDGE = 128
LANES = 128
SUB = 8
F32 = jnp.float32
BF16 = jnp.bfloat16


def sincos(turn, samples):
    quarter = samples // 4
    quadrant = (turn + quarter // 2) // quarter if quarter & (quarter - 1) else lax.shift_right_logical(
        turn + quarter // 2, jnp.full_like(turn, quarter.bit_length() - 1)
    )
    y = (turn - quadrant * quarter).astype(F32) * (2.0 * math.pi / samples)
    z = y * y
    s = y + y * z * (-1.6666654611e-1 + z * (8.3321608736e-3 - z * 1.9515295891e-4))
    c = 1.0 - 0.5 * z + z * z * (4.166664568298827e-2 + z * (-1.388731625493765e-3 + z * 2.443315711809948e-5))
    odd = (quadrant & 1) == 1
    cos_abs = jnp.where(odd, s, c)
    sin_abs = jnp.where(odd, c, s)
    cos = jnp.where(((quadrant + 1) & 2) == 2, -cos_abs, cos_abs)
    sin = jnp.where((quadrant & 2) == 2, -sin_abs, sin_abs)
    return cos, sin


def dedisperse_kernel(trials_each, bins, dm_ref, cd_ref, sp_ref, send_ref, keep_ref, ph, cdcol, y, xs, dms):
    step = pl.program_id(0)
    channels, tile = sp_ref.shape[1], sp_ref.shape[2]
    samples = 2 * bins
    half = LANES // 2
    chunks = bins // half
    chan = lax.axis_index("chan")
    block = chan * lax.axis_size("bin") + lax.axis_index("bin")

    @pl.when(step == 0)
    def _():
        if channels >= LANES:
            for k in range(channels // LANES):
                row = cd_ref[pl.ds(block * (channels // LANES) + k, 1), :]
                cdcol[pl.ds(k * LANES, LANES), :] = jnp.broadcast_to(row, (LANES, LANES)).T
            cd = cdcol[...]
        else:
            first = block * channels
            row = cd_ref[pl.ds(first // LANES, 1), :]
            cdcol[...] = jnp.broadcast_to(row, (LANES, LANES)).T
            cd = cdcol[pl.ds(pl.multiple_of(first % LANES, SUB), channels), :]
        lane = lax.broadcasted_iota(jnp.int32, cd.shape, 1)
        turn = (lane & (half - 1)) * cd - jnp.where(lane >= half, samples // 4, 0)
        u, v = sincos(turn & (samples - 1), samples)
        du, dv = sincos((half * cd) & (samples - 1), samples)
        for j in range(chunks):
            value = u
            if j == 0:
                value = jnp.where(lane == half, (1 - 2 * (cd & 1)).astype(F32), u)
            ph[:, j * LANES : (j + 1) * LANES] = value.astype(BF16)
            u, v = u * du - v * dv, v * du + u * dv
        where = lax.broadcasted_iota(jnp.int32, (SUB, LANES), 1)
        trial = ((where // (2 * trials_each)) ^ chan) * trials_each + (where & (trials_each - 1))
        dm = jnp.concatenate([dm_ref[...], dm_ref[...]], axis=1)
        dms[...] = jnp.take_along_axis(jnp.broadcast_to(dm, (SUB, LANES)), trial, axis=1)
        edge = jnp.zeros((send_ref.shape[0], EDGE), BF16)
        for ref in (send_ref, keep_ref):
            ref[:, :EDGE] = edge
            ref[:, bins + EDGE :] = edge

    lhs = jnp.concatenate([sp_ref[0], sp_ref[1]], axis=1)
    y[...] = lax.dot_general(lhs, ph[...], (((0,), (0,)), ((), ())), preferred_element_type=F32)
    dm = dms[...]
    lane = lax.broadcasted_iota(jnp.int32, (SUB, LANES), 1)
    row = lax.broadcasted_iota(jnp.int32, (SUB, LANES), 0)
    imag = (lane & trials_each) != 0

    def gather(group, _):
        base = pl.multiple_of(group * SUB, SUB)
        g = ((step * tile + base + row) * dm) & (samples - 1)
        upper = g > bins
        near = jnp.where(upper, samples - g, g)
        chunk = lax.shift_right_logical(near, jnp.full_like(near, half.bit_length() - 1)) & (chunks - 1)
        swap = imag != (g == bins)
        low = near & (half - 1)
        at_re = low + jnp.where(swap, half, 0)
        at_im = at_re ^ half
        from_re = from_im = jnp.zeros((SUB, LANES), F32)
        for j in range(chunks):
            here = chunk == j
            columns = slice(j * LANES, (j + 1) * LANES)
            got = jnp.take_along_axis(y[pl.ds(base, SUB), columns], at_re, axis=1)
            from_re = jnp.where(here, got, from_re)
            got = jnp.take_along_axis(y[pl.ds(tile + base, SUB), columns], at_im, axis=1)
            from_im = jnp.where(here, got, from_im)
        sign = jnp.where((g & (bins - 1)) == 0, 0.0, jnp.where(upper, -1.0, 1.0))
        re_weight = jnp.where(imag, -sign, 1.0)
        im_weight = jnp.where(imag, 1.0, sign)
        xs[pl.ds(base, SUB), :] = from_re * re_weight + from_im * im_weight
        return 0

    lax.fori_loop(0, tile // SUB, gather, 0)
    out = xs[...].T.astype(BF16)
    columns = pl.ds(pl.multiple_of(EDGE + step * tile, LANES), tile)
    wide = 2 * trials_each
    for k in range(LANES // wide):
        ref = (keep_ref, send_ref)[k % 2]
        ref[(k // 2) * wide : (k // 2 + 1) * wide, columns] = out[k * wide : (k + 1) * wide]


def dedisperse(spectra, dm_trials, chan_delay, trials_each):
    _, channels, bins = spectra.shape
    tile = LANES
    rows = LANES // 2
    whole = lambda shape: pl.BlockSpec(shape, lambda i: (0,) * len(shape))
    delays = chan_delay.reshape(-1, LANES)
    shape = jax.ShapeDtypeStruct((rows, bins + 2 * EDGE), BF16)
    return pl.pallas_call(
        functools.partial(dedisperse_kernel, trials_each, bins),
        grid=(bins // tile,),
        in_specs=[
            whole((1, dm_trials.shape[0])),
            whole(delays.shape),
            pl.BlockSpec((2, channels, tile), lambda i: (0, 0, i)),
        ],
        out_specs=[whole(shape.shape)] * 2,
        out_shape=[shape] * 2,
        scratch_shapes=[
            pltpu.VMEM((channels, 2 * bins), BF16),
            pltpu.VMEM((max(channels, LANES), LANES), jnp.int32),
            pltpu.VMEM((2 * tile, 2 * bins), F32),
            pltpu.VMEM((tile, LANES), F32),
            pltpu.VMEM((SUB, LANES), jnp.int32),
        ],
        compiler_params=pltpu.CompilerParams(vmem_limit_bytes=48 * 2**20),
        name="dedisperse",
    )(dm_trials.reshape(1, -1), delays, spectra)


def pick_kernel(bank_ref, ids_ref, out_ref):
    bank, taps = bank_ref.shape[1:]
    count = ids_ref.shape[1]
    rows = lax.broadcasted_iota(jnp.int32, (bank, count), 0)
    one_hot = jnp.where(rows == ids_ref[...], 1.0, 0.0).astype(BF16)
    at = lax.broadcasted_iota(jnp.int32, (taps, taps), 0)
    to = lax.broadcasted_iota(jnp.int32, (taps, taps), 1)
    flip = jnp.where(at == (to ^ 15), 1.0, 0.0).astype(BF16)
    chosen = []
    for part in range(2):
        taken = lax.dot_general(one_hot, bank_ref[part], (((0,), (0,)), ((), ())), preferred_element_type=F32)
        chosen.append(jnp.dot(taken.astype(BF16), flip, preferred_element_type=F32))
    re, im = chosen
    out_ref[:count, :taps] = re.astype(BF16)
    out_ref[:count, taps:] = (-im).astype(BF16)
    out_ref[count:, :taps] = im.astype(BF16)
    out_ref[count:, taps:] = re.astype(BF16)


def pick_templates(template_bank, template_ids):
    _, bank, taps = template_bank.shape
    count = template_ids.shape[0]
    return pl.pallas_call(
        pick_kernel,
        out_shape=jax.ShapeDtypeStruct((2 * count, 2 * taps), BF16),
        cost_estimate=pl.CostEstimate(flops=4 * count * bank * taps, bytes_accessed=2**20, transcendentals=0),
        name="pick_templates",
    )(template_bank, template_ids.reshape(1, -1))


def search_kernel(scale, taps, near_ref, far_ref, templates_ref, out_ref, signal, hankel):
    step = pl.program_id(0)
    each, count, bins = out_ref.shape
    rows, width = near_ref.shape
    trials = rows // 2

    @pl.when(step == 0)
    def _():
        total = near_ref[...].astype(F32) + far_ref[...].astype(F32)
        signal[...] = (total * scale).astype(BF16).astype(F32)

    for k in range(each):
        trial = step * each + k
        for part in range(2):
            line = signal[pl.ds(part * trials + trial, 1), :]
            skew = pltpu.roll(jnp.broadcast_to(line, (16, width)), width - 15, 1, stride=1, stride_axis=0)
            for e in range(LANES // 16):
                moved = skew if e == 0 else pltpu.roll(skew, width - 16 * e, 1)
                moved = moved.astype(BF16)
                for h in range(taps // LANES):
                    at = part * taps + h * LANES + 16 * e
                    hankel[k, at : at + 16, :] = moved[:, h * LANES : h * LANES + bins]
        response = jnp.dot(templates_ref[...], hankel[k], preferred_element_type=F32)
        re, im = response[:count], response[count:]
        out_ref[k] = (re * re + im * im).astype(BF16)


def search(near, far, templates, scale, bins):
    rows, width = near.shape
    trials = rows // 2
    taps = templates.shape[1] // 2
    count = templates.shape[0] // 2
    each = min(trials, 4)
    whole = lambda shape: pl.BlockSpec(shape, lambda i: (0,) * len(shape))
    return pl.pallas_call(
        functools.partial(search_kernel, scale, taps),
        grid=(trials // each,),
        in_specs=[whole(near.shape), whole(far.shape), whole(templates.shape)],
        out_specs=pl.BlockSpec((each, count, bins), lambda i: (i, 0, 0)),
        out_shape=jax.ShapeDtypeStruct((trials, count, bins), BF16),
        scratch_shapes=[pltpu.VMEM((rows, width), F32), pltpu.VMEM((each, 2 * taps, bins), BF16)],
        compiler_params=pltpu.CompilerParams(vmem_limit_bytes=48 * 2**20),
        name="search",
    )(near, far, templates)


def swap(cells, axis, distance):
    return lax.ppermute(cells, axis, [(i, i ^ distance) for i in range(lax.axis_size(axis))])


def local(spectra, dm_trials, chan_delay, template_bank, template_ids):
    owners, spans = lax.axis_size("chan"), lax.axis_size("bin")
    bins = spectra.shape[2]
    own_bins = bins // spans
    trials_each = dm_trials.shape[0] // owners
    scale = 1.0 / math.sqrt(chan_delay.shape[0])
    wide = 2 * trials_each
    templates = pick_templates(template_bank, template_ids)
    send, keep = dedisperse(spectra, dm_trials, chan_delay, trials_each)
    distance = 1
    while True:
        got = swap(send, "chan", distance)
        distance *= 2
        if distance == owners:
            break
        total = (keep.astype(F32) + got.astype(F32)).astype(BF16).reshape(-1, 2, wide, keep.shape[1])
        keep, send = total[:, 0].reshape(-1, keep.shape[1]), total[:, 1].reshape(-1, keep.shape[1])
    place = lax.axis_index("bin")
    part = spans // 2
    while part:
        total = (keep.astype(F32) + got.astype(F32)).astype(BF16)
        left, right = total[:, : part * own_bins + 2 * EDGE], total[:, part * own_bins :]
        upper = (place & part) != 0
        keep, send = jnp.where(upper, right, left), jnp.where(upper, left, right)
        got = swap(send, "bin", part)
        part //= 2
    return search(keep, got, templates, scale, own_bins)


def solution(mesh):
    in_specs = (P(None, ("beam", "chan", "bin"), None), P(), P(), P(), P())
    out_specs = P(("beam", "chan"), None, "bin")
    return jax.shard_map(local, mesh=mesh, in_specs=in_specs, out_specs=out_specs, check_vma=False)
```

time: 449 us -> 46.1 us (0.10)
  other arithmetic: 328 us -> 0.1 us
  waiting for transfers between devices: 57.8 us -> 6.27 us
  Pallas kernels: 0 us -> 27.8 us
  local copies, waits for them, and re-layouts: 19.5 us -> 3.55 us
  between operations: 14.1 us -> 0.05 us
  matrix products: 12.4 us -> 0 us
  loops' own time: 5.74 us -> 0 us
    while x16 -> x0, other arithmetic: 325 us -> none
    unnamed x2 -> x0, waiting for transfers between devices: 30.5 us -> none
    pallas_call x0 -> x3, Pallas kernels: none -> 27.8 us  [the longest x1 21.5 us: dedisperse(): pl.pallas_call(functools.partial(dedisperse_kernel, trials_each, bins), g...]
    all_to_all x1 -> x0, waiting for transfers between devices: 23.5 us -> none  [local(): lax.all_to_all(spectra, 'bin', split_axis=2, concat_axis=1, tiled=True)]
    conv_general_dilated x1 -> x0, matrix products: 12 us -> none  [correlate(): lax.conv_general_dilated(signal, kernel, (1,), 'VALID', dimension_numbers...]
    all_to_all x1 -> x0, starting transfers between devices: 6.32 us -> none  [local(): lax.all_to_all(spectra, 'bin', split_axis=2, concat_axis=1, tiled=True)]
    another operation x1 -> x0, loops' own time: 5.74 us -> none  [dedisperse(): lax.map(one_block, jnp.arange(bin_count // block_size, dtype=jnp.int32))]
    dynamic_slice x9 -> x0, local copies, waits for them, and re-layouts: 5.38 us -> none  [the longest x8 4.69 us: dedisperse(): lax.map(one_block, jnp.arange(bin_count // block_size, dtype=jnp.int32))]
  transfers between devices with their start and end apart: 4 -> 4, of which waited for: 3 -> 4; matrix products, arithmetic and copies ran while one was open for 0% -> 0% of each run, Pallas kernels for 0% -> 4%
where the time goes in v1:
time: 46.1 us; the launch traced here: 45.8 us
  Pallas kernels  27.8 us (60%)
  starting transfers between devices  8.1 us (18%)
  waiting for transfers between devices  6.27 us (14%)
  local copies, waits for them, and re-layouts  3.55 us (8%)
    pallas_call x1, Pallas kernels, dedisperse(): pl.pallas_call(functools.partial(dedisperse_kernel, trials_each, bins), g...  21.5 us
    ppermute x4, starting transfers between devices, swap(): lax.ppermute(cells, axis, [(i, i ^ distance) for i in range(lax.axis_size...  8.1 us
    ppermute x4, waiting for transfers between devices, swap(): lax.ppermute(cells, axis, [(i, i ^ distance) for i in range(lax.axis_size...  6.27 us
    pallas_call x1, Pallas kernels, search(): pl.pallas_call(functools.partial(search_kernel, scale, taps), grid=(trial...  4.24 us
    unnamed x8, local copies, waits for them, and re-layouts  3.55 us
    pallas_call x1, Pallas kernels, pick_templates(): pl.pallas_call(pick_kernel, out_shape=jax.ShapeDtypeStruct((2 * count, 2...  2.02 us
  transfers between devices with their start and end apart: 4, of which 4 were waited for; matrix products, arithmetic and copies ran while one was open for 0% of the time, Pallas kernels for 4%

profile of v1, /device:TPU:0, one launch (start us, length us, event | category | flops | bytes accessed | tf_op | source)
XLA Modules:
  0.0 45.8 jit_solution(17604921608175760205)
XLA Ops:
  0.0 0.0 copy-start.3
  0.0 0.7 %copy-done.3 = s32[64]{0:T(128)S(1)} copy-done((s32[64]{0:T(128)S(1)}, s32[64]{0:T(128)}, u32[]{:S(2)}) %copy-start.3) | copy-done | bytes 280
  0.7 0.0 copy-start
  0.7 1.2 %copy-done = bf16[2,256,1024]{2,1,0:T(8,128)(2,1)S(1)} copy-done((bf16[2,256,1024]{2,1,0:T(8,128)(2,1)S(1)}, bf16[2,256,1024]{2,1,0:T(8,128)(2,1)}, u32[]{:S(2)}) %copy-start) | copy-done | bytes 1048600
  1.9 0.0 copy-start.2
  1.9 0.7 %copy-done.2 = s32[4096]{0:T(1024)S(1)} copy-done((s32[4096]{0:T(1024)S(1)}, s32[4096]{0:T(1024)}, u32[]{:S(2)}) %copy-start.2) | copy-done | bytes 16408
  2.6 21.5 %dedisperse.1 = (bf16[64,1280]{1,0:T(8,128)(2,1)S(1)}, bf16[64,1280]{1,0:T(8,128)(2,1)S(1)}) custom-call(s32[1,64]{1,0:T(1,128)S(1)} %bitcast.12, s32[32,128]{1,0:T(8,128)S(1)} %bitcast.11, bf16[2,256,1024]{2,1,0:T(8,128)(2,1)S(1)} %copy-done), custom_call_target="tpu_custom_call" | custom-call | tf_op jit(solution)/shard_map/dedisperse/pallas_call | solution.py:122
  24.1 0.5 %collective-permute-start = (bf16[64,1280]{1,0:T(8,128)(2,1)S(1)}, bf16[64,1280]{1,0:T(8,128)(2,1)S(1)}, u32[]{:S(2)}, u32[]{:S(2)}) collective-permute-start(bf16[64,1280]{1,0:T(8,128)(2,1)S(1)} %get-tuple-element.8), channel_id=1, source_target_pairs={{0,1},{1,0},{2,3},{3,2},{4,5},{5,4},{6,7},{7,6},{8,9},{9,8},{10,11... | collective-permute-start | bytes 491528 | tf_op jit(solution)/shard_map/ppermute | solution.py:221
  24.6 1.0 %collective-permute-done = bf16[64,1280]{1,0:T(8,128)(2,1)S(1)} collective-permute-done((bf16[64,1280]{1,0:T(8,128)(2,1)S(1)}, bf16[64,1280]{1,0:T(8,128)(2,1)S(1)}, u32[]{:S(2)}, u32[]{:S(2)}) %collective-permute-start) | collective-permute-done | bytes 163872 | tf_op jit(solution)/shard_map/ppermute | solution.py:221
  25.7 2.9 %collective-permute-start.1 = (bf16[32,1280]{1,0:T(8,128)(2,1)S(1)}, bf16[32,1280]{1,0:T(8,128)(2,1)S(1)}, u32[]{:S(2)}, u32[]{:S(2)}) collective-permute-start(bf16[32,1280]{1,0:T(8,128)(2,1)S(1)} %slice_bitcast_fusion), channel_id=1, source_target_pairs={{0,2},{1,3},{2,0},{3,1},{4,6},{5,7},{6,4},{7,5},{8,10},{9,11},{10,... | collective-permute-start | bytes 245768 | tf_op jit(solution)/shard_map/ppermute | solution.py:221
  28.6 2.8 %collective-permute-done.1 = bf16[32,1280]{1,0:T(8,128)(2,1)S(1)} collective-permute-done((bf16[32,1280]{1,0:T(8,128)(2,1)S(1)}, bf16[32,1280]{1,0:T(8,128)(2,1)S(1)}, u32[]{:S(2)}, u32[]{:S(2)}) %collective-permute-start.1) | collective-permute-done | bytes 81952 | tf_op jit(solution)/shard_map/ppermute | solution.py:221
  31.4 2.9 %collective-permute-start.2 = (bf16[32,768]{1,0:T(8,128)(2,1)S(1)}, bf16[32,768]{1,0:T(8,128)(2,1)S(1)}, u32[]{:S(2)}, u32[]{:S(2)}) collective-permute-start(bf16[32,768]{1,0:T(8,128)(2,1)S(1)} %broadcast_select_fusion), channel_id=1, source_target_pairs={{0,8},{4,12},{8,0},{12,4},{1,9},{5,13},{9,1},{13,5},{2,10},{6,14},... | collective-permute-start | bytes 147464 | tf_op jit(solution)/shard_map/ppermute | solution.py:221
  34.3 2.3 %collective-permute-done.2 = bf16[32,768]{1,0:T(8,128)(2,1)S(1)} collective-permute-done((bf16[32,768]{1,0:T(8,128)(2,1)S(1)}, bf16[32,768]{1,0:T(8,128)(2,1)S(1)}, u32[]{:S(2)}, u32[]{:S(2)}) %collective-permute-start.2) | collective-permute-done | bytes 49184 | tf_op jit(solution)/shard_map/ppermute | solution.py:221
  36.7 1.8 %collective-permute-start.3 = (bf16[32,512]{1,0:T(8,128)(2,1)S(1)}, bf16[32,512]{1,0:T(8,128)(2,1)S(1)}, u32[]{:S(2)}, u32[]{:S(2)}) collective-permute-start(bf16[32,512]{1,0:T(8,128)(2,1)S(1)} %get-tuple-element.9), channel_id=1, source_target_pairs={{0,4},{4,0},{8,12},{12,8},{1,5},{5,1},{9,13},{13,9},{2,6},{6,2},{1... | collective-permute-start | bytes 98312 | tf_op jit(solution)/shard_map/ppermute | solution.py:221
  38.4 2.0 %pick_templates.1.templates_ref = bf16[256,512]{1,0:T(8,128)(2,1)} custom-call(bf16[2,256,256]{2,1,0:T(8,128)(2,1)} %bank_ref.1, s32[1,128]{1,0:T(1,128)} %bitcast.15), custom_call_target="tpu_custom_call" | custom-call | flops 33554432 | bytes 1048576 | tf_op jit(solution)/shard_map/pick_templates/pallas_call | solution.py:166
  40.4 0.2 collective-permute-done.3.far_ref
  40.6 0.0 copy-start.1
  40.6 0.9 %copy-done.1 = bf16[256,512]{1,0:T(8,128)(2,1)S(1)} copy-done((bf16[256,512]{1,0:T(8,128)(2,1)S(1)}, bf16[256,512]{1,0:T(8,128)(2,1)}, u32[]{:S(2)}) %copy-start.1) | copy-done | bytes 262168
  41.6 4.2 %search.1 = bf16[16,128,256]{2,1,0:T(8,128)(2,1)} custom-call(bf16[32,512]{1,0:T(8,128)(2,1)S(1)} %get-tuple-element.10.near_ref, bf16[32,512]{1,0:T(8,128)(2,1)S(1)} %collective-permute-done.3.far_ref, bf16[256,512]{1,0:T(8,128)(2,1)S(1)} %copy-done.1), custom_call_target="tpu_custom_call" | custom-call | tf_op jit(solution)/shard_map/search/pallas_call | solution.py:208
  (6 shorter events, 0.1 us)
Async XLA Ops:
  0.0 0.7 %copy-start.3 = (s32[64]{0:T(128)S(1)}, s32[64]{0:T(128)}, u32[]{:S(2)}) copy-start(s32[64]{0:T(128)} %param.6) | copy-start | bytes 772
  0.7 1.2 %copy-start = (bf16[2,256,1024]{2,1,0:T(8,128)(2,1)S(1)}, bf16[2,256,1024]{2,1,0:T(8,128)(2,1)}, u32[]{:S(2)}) copy-start(bf16[2,256,1024]{2,1,0:T(8,128)(2,1)} %sp_ref.1) | copy-start | bytes 3145732
  1.9 0.7 %copy-start.2 = (s32[4096]{0:T(1024)S(1)}, s32[4096]{0:T(1024)}, u32[]{:S(2)}) copy-start(s32[4096]{0:T(1024)} %param.7) | copy-start | bytes 49156
  24.1 1.5 %collective-permute-start = (bf16[64,1280]{1,0:T(8,128)(2,1)S(1)}, bf16[64,1280]{1,0:T(8,128)(2,1)S(1)}, u32[]{:S(2)}, u32[]{:S(2)}) collective-permute-start(bf16[64,1280]{1,0:T(8,128)(2,1)S(1)} %get-tuple-element.8), channel_id=1, source_target_pairs={{0,1},{1,0},{2,3},{3,2},{4,5},{5,4},{6,7},{7,6},{8,9},{9,8},{10,11... | collective-permute-start | bytes 491528 | tf_op jit(solution)/shard_map/ppermute | solution.py:221
  25.7 5.7 %collective-permute-start.1 = (bf16[32,1280]{1,0:T(8,128)(2,1)S(1)}, bf16[32,1280]{1,0:T(8,128)(2,1)S(1)}, u32[]{:S(2)}, u32[]{:S(2)}) collective-permute-start(bf16[32,1280]{1,0:T(8,128)(2,1)S(1)} %slice_bitcast_fusion), channel_id=1, source_target_pairs={{0,2},{1,3},{2,0},{3,1},{4,6},{5,7},{6,4},{7,5},{8,10},{9,11},{10,... | collective-permute-start | bytes 245768 | tf_op jit(solution)/shard_map/ppermute | solution.py:221
  31.4 5.2 %collective-permute-start.2 = (bf16[32,768]{1,0:T(8,128)(2,1)S(1)}, bf16[32,768]{1,0:T(8,128)(2,1)S(1)}, u32[]{:S(2)}, u32[]{:S(2)}) collective-permute-start(bf16[32,768]{1,0:T(8,128)(2,1)S(1)} %broadcast_select_fusion), channel_id=1, source_target_pairs={{0,8},{4,12},{8,0},{12,4},{1,9},{5,13},{9,1},{13,5},{2,10},{6,14},... | collective-permute-start | bytes 147464 | tf_op jit(solution)/shard_map/ppermute | solution.py:221
  36.7 4.0 %collective-permute-start.3 = (bf16[32,512]{1,0:T(8,128)(2,1)S(1)}, bf16[32,512]{1,0:T(8,128)(2,1)S(1)}, u32[]{:S(2)}, u32[]{:S(2)}) collective-permute-start(bf16[32,512]{1,0:T(8,128)(2,1)S(1)} %get-tuple-element.9), channel_id=1, source_target_pairs={{0,4},{4,0},{8,12},{12,8},{1,5},{5,1},{9,13},{13,9},{2,6},{6,2},{1... | collective-permute-start | bytes 98312 | tf_op jit(solution)/shard_map/ppermute | solution.py:221
  40.6 1.0 %copy-start.1 = (bf16[256,512]{1,0:T(8,128)(2,1)S(1)}, bf16[256,512]{1,0:T(8,128)(2,1)}, u32[]{:S(2)}) copy-start(bf16[256,512]{1,0:T(8,128)(2,1)} %pick_templates.1.templates_ref) | copy-start | bytes 786436

commit v2 on v1

--- a/solution.py
+++ b/solution.py
@@ -32,111 +32,204 @@
     return cos, sin
 
 
-def dedisperse_kernel(trials_each, bins, dm_ref, cd_ref, sp_ref, send_ref, keep_ref, ph, cdcol, y, xs, dms):
-    step = pl.program_id(0)
-    channels, tile = sp_ref.shape[1], sp_ref.shape[2]
+def repeat(count, body):
+    if count <= 8:
+        for i in range(count):
+            body(i)
+    else:
+        lax.fori_loop(0, count, lambda i, carry: (body(i), carry)[1], 0)
+
+
+def multiple(value, of):
+    return value if isinstance(value, int) else pl.multiple_of(value, of)
+
+
+def lane_gather(values, at):
+    dims = lax.GatherDimensionNumbers(
+        offset_dims=(),
+        collapsed_slice_dims=(1,),
+        start_index_map=(1,),
+        operand_batching_dims=(0,),
+        start_indices_batching_dims=(0,),
+    )
+    return lax.gather(values, at[..., None], dims, (1, 1), mode=lax.GatherScatterMode.PROMISE_IN_BOUNDS)
+
+
+def iota(shape, dim):
+    return lax.broadcasted_iota(jnp.int32, shape, dim)
+
+
+def shift(values, by):
+    return lax.shift_right_logical(values, jnp.full_like(values, by))
+
+
+STEP, FIRST = (2, 4, 8, 8), (1, 2, 4, 0)
+RESIDUES = (0, 4, 2, 6, 1, 5, 3, 7)
+
+
+def class_order():
+    row, column = iota((LANES, LANES), 0), iota((LANES, LANES), 1)
+    bin_of, first = jnp.full_like(row, 0), 0
+    for step, start in zip(STEP, FIRST):
+        bin_of = jnp.where(row >= first, step * (row - first) + start, bin_of)
+        first += LANES // step
+    return jnp.where(bin_of == column, 1.0, 0.0).astype(BF16)
+
+
+def dedisperse_kernel(trials_each, dm_ref, cd_ref, sp_hbm, send_ref, keep_ref, sp, ph, turned, y0, y1, xs, sem):
+    channels, bins = sp.shape[1:]
     samples = 2 * bins
     half = LANES // 2
-    chunks = bins // half
+    tiles = bins // LANES
+    spread = bins // (8 * half)
+    chunks = 8 * spread
     chan = lax.axis_index("chan")
     block = chan * lax.axis_size("bin") + lax.axis_index("bin")
-
-    @pl.when(step == 0)
-    def _():
-        if channels >= LANES:
-            for k in range(channels // LANES):
-                row = cd_ref[pl.ds(block * (channels // LANES) + k, 1), :]
-                cdcol[pl.ds(k * LANES, LANES), :] = jnp.broadcast_to(row, (LANES, LANES)).T
-            cd = cdcol[...]
-        else:
-            first = block * channels
-            row = cd_ref[pl.ds(first // LANES, 1), :]
-            cdcol[...] = jnp.broadcast_to(row, (LANES, LANES)).T
-            cd = cdcol[pl.ds(pl.multiple_of(first % LANES, SUB), channels), :]
-        lane = lax.broadcasted_iota(jnp.int32, cd.shape, 1)
-        turn = (lane & (half - 1)) * cd - jnp.where(lane >= half, samples // 4, 0)
-        u, v = sincos(turn & (samples - 1), samples)
-        du, dv = sincos((half * cd) & (samples - 1), samples)
-        for j in range(chunks):
+    fetch = pltpu.make_async_copy(sp_hbm, sp, sem)
+    fetch.start()
+
+    if channels >= LANES:
+        rows = [cd_ref[pl.ds(block * (channels // LANES) + k, 1), :] for k in range(channels // LANES)]
+        cd = jnp.concatenate([jnp.broadcast_to(row, (LANES, LANES)).T for row in rows], axis=0)
+    else:
+        first = block * channels
+        row = cd_ref[pl.ds(first // LANES, 1), :]
+        moved = pltpu.roll(jnp.broadcast_to(row, (LANES, LANES)), (LANES - first % LANES) % LANES, 1)
+        cd = moved.T[:channels]
+    lane = iota(cd.shape, 1)
+    start = 8 * (lane & (half - 1)) * cd - jnp.where(lane >= half, samples // 4, 0)
+    du, dv = sincos(cd & (samples - 1), samples)
+    for h in range(spread):
+        u, v = sincos((start + 8 * half * h * cd) & (samples - 1), samples)
+        for residue in range(8):
             value = u
-            if j == 0:
+            if h == 0 and residue == 0:
                 value = jnp.where(lane == half, (1 - 2 * (cd & 1)).astype(F32), u)
-            ph[:, j * LANES : (j + 1) * LANES] = value.astype(BF16)
-            u, v = u * du - v * dv, v * du + u * dv
-        where = lax.broadcasted_iota(jnp.int32, (SUB, LANES), 1)
-        trial = ((where // (2 * trials_each)) ^ chan) * trials_each + (where & (trials_each - 1))
-        dm = jnp.concatenate([dm_ref[...], dm_ref[...]], axis=1)
-        dms[...] = jnp.take_along_axis(jnp.broadcast_to(dm, (SUB, LANES)), trial, axis=1)
-        edge = jnp.zeros((send_ref.shape[0], EDGE), BF16)
-        for ref in (send_ref, keep_ref):
-            ref[:, :EDGE] = edge
-            ref[:, bins + EDGE :] = edge
-
-    lhs = jnp.concatenate([sp_ref[0], sp_ref[1]], axis=1)
-    y[...] = lax.dot_general(lhs, ph[...], (((0,), (0,)), ((), ())), preferred_element_type=F32)
-    dm = dms[...]
-    lane = lax.broadcasted_iota(jnp.int32, (SUB, LANES), 1)
-    row = lax.broadcasted_iota(jnp.int32, (SUB, LANES), 0)
+            at = (RESIDUES.index(residue) * spread + h) * LANES
+            ph[:, at : at + LANES] = value.astype(BF16)
+            if residue < 7:
+                u, v = u * du - v * dv, v * du + u * dv
+
+    lane = iota((16, LANES), 1)
+    trial = ((lane // (2 * trials_each)) ^ chan) * trials_each + (lane & (trials_each - 1))
+    dm = jnp.concatenate([dm_ref[...], dm_ref[...]], axis=1)
+    dm = jnp.take_along_axis(jnp.broadcast_to(dm, (16, LANES)), trial, axis=1)
     imag = (lane & trials_each) != 0
-
-    def gather(group, _):
-        base = pl.multiple_of(group * SUB, SUB)
-        g = ((step * tile + base + row) * dm) & (samples - 1)
-        upper = g > bins
-        near = jnp.where(upper, samples - g, g)
-        chunk = lax.shift_right_logical(near, jnp.full_like(near, half.bit_length() - 1)) & (chunks - 1)
-        swap = imag != (g == bins)
-        low = near & (half - 1)
-        at_re = low + jnp.where(swap, half, 0)
-        at_im = at_re ^ half
-        from_re = from_im = jnp.zeros((SUB, LANES), F32)
-        for j in range(chunks):
-            here = chunk == j
-            columns = slice(j * LANES, (j + 1) * LANES)
-            got = jnp.take_along_axis(y[pl.ds(base, SUB), columns], at_re, axis=1)
-            from_re = jnp.where(here, got, from_re)
-            got = jnp.take_along_axis(y[pl.ds(tile + base, SUB), columns], at_im, axis=1)
-            from_im = jnp.where(here, got, from_im)
-        sign = jnp.where((g & (bins - 1)) == 0, 0.0, jnp.where(upper, -1.0, 1.0))
-        re_weight = jnp.where(imag, -sign, 1.0)
-        im_weight = jnp.where(imag, 1.0, sign)
-        xs[pl.ds(base, SUB), :] = from_re * re_weight + from_im * im_weight
-        return 0
-
-    lax.fori_loop(0, tile // SUB, gather, 0)
-    out = xs[...].T.astype(BF16)
-    columns = pl.ds(pl.multiple_of(EDGE + step * tile, LANES), tile)
+    row = iota((16, LANES), 0)
+    own_half = jnp.where(imag, half, 0)
+    edge = jnp.zeros((send_ref.shape[0], EDGE), BF16)
+    for ref in (send_ref, keep_ref):
+        ref[:, :EDGE] = edge
+        ref[:, bins + EDGE :] = edge
+
+    order = class_order()
+    fetch.wait()
+    starts = [sum(bins // s for s in STEP[:k]) for k in range(4)]
+
+    def turn_tile(t):
+        columns = pl.ds(multiple(t * LANES, LANES), LANES)
+        for part in range(2):
+            rows = lax.dot_general(order, sp[part, :, columns], (((1,), (1,)), ((), ())), preferred_element_type=F32)
+            rows = rows.astype(BF16)
+            first = 0
+            for k in range(4):
+                size = LANES // STEP[k]
+                turned[part, pl.ds(multiple(starts[k] + t * size, 16), size), :] = rows[first : first + size]
+                first += size
+
+    repeat(tiles, turn_tile)
+
+    def multiply(k, b, size, y):
+        count = chunks >> k
+        columns = count * LANES
+        rows = pl.ds(multiple(starts[k] + b * size, 16), size)
+        for part in range(2):
+            y[part, :size, :columns] = jnp.dot(
+                turned[part, rows, :], ph[:, :columns], preferred_element_type=F32
+            ).astype(BF16)
+
+    def pick(k, b, size, y):
+        each = LANES // STEP[k]
+        tile_first = sum(LANES // s for s in STEP[:k])
+
+        def group(i):
+            base = b * size + i * 16
+            signed = ((STEP[k] * (base + row) + FIRST[k]) * dm + bins & (samples - 1)) - bins
+            near = jnp.abs(signed)
+            key = (near & (bins - 1 - 8 * (half - 1))).astype(jnp.int16)
+            at_re = (shift(near, 3) & (half - 1)) ^ own_half ^ jnp.where(signed == -bins, half, 0)
+            at_im = (at_re ^ half).astype(jnp.int16)
+            at_re = at_re.astype(jnp.int16)
+            got = []
+            for part, at in ((0, at_re), (1, at_im)):
+                value = None
+                for j in range(chunks >> k):
+                    lanes = slice(j * LANES, (j + 1) * LANES)
+                    new = lane_gather(y[part, pl.ds(multiple(i * 16, 16), 16), lanes], at)
+                    this = RESIDUES[j // spread] + 8 * half * (j % spread)
+                    value = new if value is None else jnp.where(key == this, new, value)
+                got.append(value.astype(F32))
+            sign = jnp.where((signed & (bins - 1)) == 0, 0.0, jnp.where(signed < 0, -1.0, 1.0))
+            total = got[0] * jnp.where(imag, -sign, 1.0) + got[1] * jnp.where(imag, 1.0, sign)
+            at = (base // each) * LANES + tile_first + base % each
+            xs[pl.ds(multiple(at, 16), 16), :] = total.astype(BF16)
+
+        repeat(size // 16, group)
+
+    size = y0.shape[1]
+    work = [(k, b, min(size, bins // STEP[k])) for k in range(4) for b in range(max(1, bins // STEP[k] // size))]
+    if len(work) <= 16:
+        buffers = (y0, y1)
+        multiply(*work[0], y0)
+        for n, item in enumerate(work):
+            if n + 1 < len(work):
+                multiply(*work[n + 1], buffers[(n + 1) % 2])
+            pick(*item, buffers[n % 2])
+    else:
+        for k in range(4):
+
+            def whole_block(b, carry, k=k):
+                multiply(k, b, min(size, bins // STEP[k]), y0)
+                pick(k, b, min(size, bins // STEP[k]), y0)
+                return carry
+
+            lax.fori_loop(0, max(1, bins // STEP[k] // size), whole_block, 0)
+
     wide = 2 * trials_each
-    for k in range(LANES // wide):
-        ref = (keep_ref, send_ref)[k % 2]
-        ref[(k // 2) * wide : (k // 2 + 1) * wide, columns] = out[k * wide : (k + 1) * wide]
+
+    def finish(t):
+        rows = xs[pl.ds(multiple(t * LANES, LANES), LANES), :]
+        out = lax.dot_general(rows, order, (((0,), (0,)), ((), ())), preferred_element_type=F32).astype(BF16)
+        columns = pl.ds(multiple(EDGE + t * LANES, LANES), LANES)
+        for k in range(LANES // wide):
+            ref = (keep_ref, send_ref)[k % 2]
+            ref[(k // 2) * wide : (k // 2 + 1) * wide, columns] = out[k * wide : (k + 1) * wide]
+
+    repeat(tiles, finish)
 
 
 def dedisperse(spectra, dm_trials, chan_delay, trials_each):
     _, channels, bins = spectra.shape
-    tile = LANES
+    size = 128
     rows = LANES // 2
-    whole = lambda shape: pl.BlockSpec(shape, lambda i: (0,) * len(shape))
     delays = chan_delay.reshape(-1, LANES)
     shape = jax.ShapeDtypeStruct((rows, bins + 2 * EDGE), BF16)
+    in_vmem = pl.BlockSpec(memory_space=pltpu.VMEM)
     return pl.pallas_call(
-        functools.partial(dedisperse_kernel, trials_each, bins),
-        grid=(bins // tile,),
-        in_specs=[
-            whole((1, dm_trials.shape[0])),
-            whole(delays.shape),
-            pl.BlockSpec((2, channels, tile), lambda i: (0, 0, i)),
-        ],
-        out_specs=[whole(shape.shape)] * 2,
+        functools.partial(dedisperse_kernel, trials_each),
+        in_specs=[in_vmem, in_vmem, pl.BlockSpec(memory_space=pl.ANY)],
+        out_specs=[in_vmem] * 2,
         out_shape=[shape] * 2,
         scratch_shapes=[
+            pltpu.VMEM(spectra.shape, BF16),
             pltpu.VMEM((channels, 2 * bins), BF16),
-            pltpu.VMEM((max(channels, LANES), LANES), jnp.int32),
-            pltpu.VMEM((2 * tile, 2 * bins), F32),
-            pltpu.VMEM((tile, LANES), F32),
-            pltpu.VMEM((SUB, LANES), jnp.int32),
+            pltpu.VMEM((2, bins, channels), BF16),
+            pltpu.VMEM((2, size, 2 * bins), BF16),
+            pltpu.VMEM((2, size, 2 * bins), BF16),
+            pltpu.VMEM((bins, LANES), BF16),
+            pltpu.SemaphoreType.DMA,
         ],
-        compiler_params=pltpu.CompilerParams(vmem_limit_bytes=48 * 2**20),
+        compiler_params=pltpu.CompilerParams(vmem_limit_bytes=62 * 2**20),
         name="dedisperse",
     )(dm_trials.reshape(1, -1), delays, spectra)
 

time: 46.1 us -> 29.7 us (0.64)
  Pallas kernels: 27.8 us -> 12.8 us
  local copies, waits for them, and re-layouts: 3.55 us -> 0.96 us
  other arithmetic: 0.1 us -> 1.03 us
    pallas_call x1, Pallas kernels: 21.5 us -> 6.56 us  [dedisperse(): pl.pallas_call(functools.partial(dedisperse_kernel, trials_each), in_spec...]
    unnamed x8 -> x2, local copies, waits for them, and re-layouts: 3.55 us -> 0.95 us
    convert_element_type x1, other arithmetic: 0.04 us -> 0.96 us  [local(): (keep.astype(F32) + got.astype(F32)).astype(BF16)]
  transfers between devices with their start and end apart: 4 -> 4, of which waited for: 4 -> 4; matrix products, arithmetic and copies ran while one was open for 0% -> 0% of each run, Pallas kernels for 4% -> 7%
where the time goes in v2:
time: 29.7 us; the launch traced here: 29.4 us
  Pallas kernels  12.8 us (43%)
  starting transfers between devices  8.1 us (27%)
  waiting for transfers between devices  6.48 us (22%)
  other arithmetic  1.03 us (3%)
  local copies, waits for them, and re-layouts  0.96 us (3%)
    ppermute x4, starting transfers between devices, swap(): lax.ppermute(cells, axis, [(i, i ^ distance) for i in range(lax.axis_size...  8.1 us
    pallas_call x1, Pallas kernels, dedisperse(): pl.pallas_call(functools.partial(dedisperse_kernel, trials_each), in_spec...  6.56 us
    ppermute x4, waiting for transfers between devices, swap(): lax.ppermute(cells, axis, [(i, i ^ distance) for i in range(lax.axis_size...  6.48 us
    pallas_call x1, Pallas kernels, search(): pl.pallas_call(functools.partial(search_kernel, scale, taps), grid=(trial...  4.24 us
    pallas_call x1, Pallas kernels, pick_templates(): pl.pallas_call(pick_kernel, out_shape=jax.ShapeDtypeStruct((2 * count, 2...  2.02 us
    convert_element_type x1, other arithmetic, local(): (keep.astype(F32) + got.astype(F32)).astype(BF16)  0.96 us
    unnamed x2, local copies, waits for them, and re-layouts  0.95 us
  transfers between devices with their start and end apart: 4, of which 4 were waited for; matrix products, arithmetic and copies ran while one was open for 0% of the time, Pallas kernels for 7%

profile of v2, /device:TPU:0, one launch (start us, length us, event | category | flops | bytes accessed | tf_op | source)
XLA Modules:
  0.0 29.4 jit_solution(13189834011160651323)
XLA Ops:
  0.0 6.6 %dedisperse.1 = (bf16[64,1280]{1,0:T(8,128)(2,1)}, bf16[64,1280]{1,0:T(8,128)(2,1)}) custom-call(s32[1,64]{1,0:T(1,128)} %bitcast.14, s32[32,128]{1,0:T(8,128)} %bitcast.13, bf16[2,256,1024]{2,1,0:T(8,128)(2,1)} %sp_hbm.1), custom_call_target="tpu_custom_call" | custom-call | tf_op jit(solution)/shard_map/dedisperse/pallas_call | solution.py:218
  6.6 0.5 %collective-permute-start = (bf16[64,1280]{1,0:T(8,128)(2,1)}, bf16[64,1280]{1,0:T(8,128)(2,1)S(1)}, u32[]{:S(2)}, u32[]{:S(2)}) collective-permute-start(bf16[64,1280]{1,0:T(8,128)(2,1)} %get-tuple-element.8), channel_id=1, source_target_pairs={{0,1},{1,0},{2,3},{3,2},{4,5},{5,4},{6,7},{7,6},{8,9},{9,8},{10,11... | collective-permute-start | bytes 491528 | tf_op jit(solution)/shard_map/ppermute | solution.py:314
  7.1 1.2 %collective-permute-done = bf16[64,1280]{1,0:T(8,128)(2,1)S(1)} collective-permute-done((bf16[64,1280]{1,0:T(8,128)(2,1)}, bf16[64,1280]{1,0:T(8,128)(2,1)S(1)}, u32[]{:S(2)}, u32[]{:S(2)}) %collective-permute-start) | collective-permute-done | bytes 163872 | tf_op jit(solution)/shard_map/ppermute | solution.py:314
  8.3 1.0 %add_convert_fusion = bf16[64,1280]{1,0:T(8,128)(2,1)S(1)} fusion(bf16[64,1280]{1,0:T(8,128)(2,1)S(1)} %collective-permute-done, bf16[64,1280]{1,0:T(8,128)(2,1)} %get-tuple-element.7), kind=kLoop, calls=%fused_computation | loop fusion | flops 327680 | bytes 491520 | tf_op jit(solution)/shard_map/convert_element_type | solution.py:332
  9.3 2.9 %collective-permute-start.1 = (bf16[32,1280]{1,0:T(8,128)(2,1)S(1)}, bf16[32,1280]{1,0:T(8,128)(2,1)S(1)}, u32[]{:S(2)}, u32[]{:S(2)}) collective-permute-start(bf16[32,1280]{1,0:T(8,128)(2,1)S(1)} %slice_bitcast_fusion), channel_id=1, source_target_pairs={{0,2},{1,3},{2,0},{3,1},{4,6},{5,7},{6,4},{7,5},{8,10},{9,11},{10,... | collective-permute-start | bytes 245768 | tf_op jit(solution)/shard_map/ppermute | solution.py:314
  12.2 2.8 %collective-permute-done.1 = bf16[32,1280]{1,0:T(8,128)(2,1)S(1)} collective-permute-done((bf16[32,1280]{1,0:T(8,128)(2,1)S(1)}, bf16[32,1280]{1,0:T(8,128)(2,1)S(1)}, u32[]{:S(2)}, u32[]{:S(2)}) %collective-permute-start.1) | collective-permute-done | bytes 81952 | tf_op jit(solution)/shard_map/ppermute | solution.py:314
  15.0 2.9 %collective-permute-start.2 = (bf16[32,768]{1,0:T(8,128)(2,1)S(1)}, bf16[32,768]{1,0:T(8,128)(2,1)S(1)}, u32[]{:S(2)}, u32[]{:S(2)}) collective-permute-start(bf16[32,768]{1,0:T(8,128)(2,1)S(1)} %broadcast_select_fusion), channel_id=1, source_target_pairs={{0,8},{4,12},{8,0},{12,4},{1,9},{5,13},{9,1},{13,5},{2,10},{6,14},... | collective-permute-start | bytes 147464 | tf_op jit(solution)/shard_map/ppermute | solution.py:314
  17.9 2.3 %collective-permute-done.2 = bf16[32,768]{1,0:T(8,128)(2,1)S(1)} collective-permute-done((bf16[32,768]{1,0:T(8,128)(2,1)S(1)}, bf16[32,768]{1,0:T(8,128)(2,1)S(1)}, u32[]{:S(2)}, u32[]{:S(2)}) %collective-permute-start.2) | collective-permute-done | bytes 49184 | tf_op jit(solution)/shard_map/ppermute | solution.py:314
  20.2 1.8 %collective-permute-start.3 = (bf16[32,512]{1,0:T(8,128)(2,1)S(1)}, bf16[32,512]{1,0:T(8,128)(2,1)S(1)}, u32[]{:S(2)}, u32[]{:S(2)}) collective-permute-start(bf16[32,512]{1,0:T(8,128)(2,1)S(1)} %get-tuple-element.9), channel_id=1, source_target_pairs={{0,4},{4,0},{8,12},{12,8},{1,5},{5,1},{9,13},{13,9},{2,6},{6,2},{1... | collective-permute-start | bytes 98312 | tf_op jit(solution)/shard_map/ppermute | solution.py:314
  22.0 2.0 %pick_templates.1.templates_ref = bf16[256,512]{1,0:T(8,128)(2,1)} custom-call(bf16[2,256,256]{2,1,0:T(8,128)(2,1)} %bank_ref.1, s32[1,128]{1,0:T(1,128)} %bitcast.15), custom_call_target="tpu_custom_call" | custom-call | flops 33554432 | bytes 1048576 | tf_op jit(solution)/shard_map/pick_templates/pallas_call | solution.py:259
  24.0 0.2 collective-permute-done.3.far_ref
  24.2 0.0 copy-start
  24.2 0.9 %copy-done = bf16[256,512]{1,0:T(8,128)(2,1)S(1)} copy-done((bf16[256,512]{1,0:T(8,128)(2,1)S(1)}, bf16[256,512]{1,0:T(8,128)(2,1)}, u32[]{:S(2)}) %copy-start) | copy-done | bytes 262168
  25.2 4.2 %search.1 = bf16[16,128,256]{2,1,0:T(8,128)(2,1)} custom-call(bf16[32,512]{1,0:T(8,128)(2,1)S(1)} %get-tuple-element.10.near_ref, bf16[32,512]{1,0:T(8,128)(2,1)S(1)} %collective-permute-done.3.far_ref, bf16[256,512]{1,0:T(8,128)(2,1)S(1)} %copy-done), custom_call_target="tpu_custom_call" | custom-call | tf_op jit(solution)/shard_map/search/pallas_call | solution.py:301
  (5 shorter events, 0.1 us)
Async XLA Ops:
  6.6 1.8 %collective-permute-start = (bf16[64,1280]{1,0:T(8,128)(2,1)}, bf16[64,1280]{1,0:T(8,128)(2,1)S(1)}, u32[]{:S(2)}, u32[]{:S(2)}) collective-permute-start(bf16[64,1280]{1,0:T(8,128)(2,1)} %get-tuple-element.8), channel_id=1, source_target_pairs={{0,1},{1,0},{2,3},{3,2},{4,5},{5,4},{6,7},{7,6},{8,9},{9,8},{10,11... | collective-permute-start | bytes 491528 | tf_op jit(solution)/shard_map/ppermute | solution.py:314
  9.3 5.7 %collective-permute-start.1 = (bf16[32,1280]{1,0:T(8,128)(2,1)S(1)}, bf16[32,1280]{1,0:T(8,128)(2,1)S(1)}, u32[]{:S(2)}, u32[]{:S(2)}) collective-permute-start(bf16[32,1280]{1,0:T(8,128)(2,1)S(1)} %slice_bitcast_fusion), channel_id=1, source_target_pairs={{0,2},{1,3},{2,0},{3,1},{4,6},{5,7},{6,4},{7,5},{8,10},{9,11},{10,... | collective-permute-start | bytes 245768 | tf_op jit(solution)/shard_map/ppermute | solution.py:314
  15.0 5.2 %collective-permute-start.2 = (bf16[32,768]{1,0:T(8,128)(2,1)S(1)}, bf16[32,768]{1,0:T(8,128)(2,1)S(1)}, u32[]{:S(2)}, u32[]{:S(2)}) collective-permute-start(bf16[32,768]{1,0:T(8,128)(2,1)S(1)} %broadcast_select_fusion), channel_id=1, source_target_pairs={{0,8},{4,12},{8,0},{12,4},{1,9},{5,13},{9,1},{13,5},{2,10},{6,14},... | collective-permute-start | bytes 147464 | tf_op jit(solution)/shard_map/ppermute | solution.py:314
  20.2 4.0 %collective-permute-start.3 = (bf16[32,512]{1,0:T(8,128)(2,1)S(1)}, bf16[32,512]{1,0:T(8,128)(2,1)S(1)}, u32[]{:S(2)}, u32[]{:S(2)}) collective-permute-start(bf16[32,512]{1,0:T(8,128)(2,1)S(1)} %get-tuple-element.9), channel_id=1, source_target_pairs={{0,4},{4,0},{8,12},{12,8},{1,5},{5,1},{9,13},{13,9},{2,6},{6,2},{1... | collective-permute-start | bytes 98312 | tf_op jit(solution)/shard_map/ppermute | solution.py:314
  24.2 1.0 %copy-start = (bf16[256,512]{1,0:T(8,128)(2,1)S(1)}, bf16[256,512]{1,0:T(8,128)(2,1)}, u32[]{:S(2)}) copy-start(bf16[256,512]{1,0:T(8,128)(2,1)} %pick_templates.1.templates_ref) | copy-start | bytes 786436

commit v3 on v2

--- a/solution.py
+++ b/solution.py
@@ -76,7 +76,13 @@
     return jnp.where(bin_of == column, 1.0, 0.0).astype(BF16)
 
 
-def dedisperse_kernel(trials_each, dm_ref, cd_ref, sp_hbm, send_ref, keep_ref, sp, ph, turned, y0, y1, xs, sem):
+def times(one, other):
+    return one[0] * other[0] - one[1] * other[1], one[1] * other[0] + one[0] * other[1]
+
+
+def dedisperse_kernel(
+    trials_each, dm_hbm, cd_hbm, sp_hbm, send_ref, keep_ref, dm_ref, cd_ref, sp, ph, turned, y0, y1, xs, sems
+):
     channels, bins = sp.shape[1:]
     samples = 2 * bins
     half = LANES // 2
@@ -85,9 +91,19 @@
     chunks = 8 * spread
     chan = lax.axis_index("chan")
     block = chan * lax.axis_size("bin") + lax.axis_index("bin")
-    fetch = pltpu.make_async_copy(sp_hbm, sp, sem)
-    fetch.start()
-
+    fetches = [
+        pltpu.make_async_copy(source, target, sems.at[n])
+        for n, (source, target) in enumerate(((cd_hbm, cd_ref), (sp_hbm, sp), (dm_hbm, dm_ref)))
+    ]
+    for fetch in fetches:
+        fetch.start()
+    order = class_order()
+    edge = jnp.zeros((send_ref.shape[0], EDGE), BF16)
+    for ref in (send_ref, keep_ref):
+        ref[:, :EDGE] = edge
+        ref[:, bins + EDGE :] = edge
+
+    fetches[0].wait()
     if channels >= LANES:
         rows = [cd_ref[pl.ds(block * (channels // LANES) + k, 1), :] for k in range(channels // LANES)]
         cd = jnp.concatenate([jnp.broadcast_to(row, (LANES, LANES)).T for row in rows], axis=0)
@@ -96,20 +112,27 @@
         row = cd_ref[pl.ds(first // LANES, 1), :]
         moved = pltpu.roll(jnp.broadcast_to(row, (LANES, LANES)), (LANES - first % LANES) % LANES, 1)
         cd = moved.T[:channels]
-    lane = iota(cd.shape, 1)
-    start = 8 * (lane & (half - 1)) * cd - jnp.where(lane >= half, samples // 4, 0)
-    du, dv = sincos(cd & (samples - 1), samples)
-    for h in range(spread):
-        u, v = sincos((start + 8 * half * h * cd) & (samples - 1), samples)
-        for residue in range(8):
-            value = u
+    column = iota(cd.shape, 1)
+    start = 8 * (column & (half - 1)) * cd - jnp.where(column >= half, samples // 4, 0)
+    turns = {1: sincos(cd & (samples - 1), samples)}
+    turns[2] = times(turns[1], turns[1])
+    turns[4] = times(turns[2], turns[2])
+    bases = [{0: sincos((start + 8 * half * h * cd) & (samples - 1), samples)} for h in range(spread)]
+
+    def make_phases(residue):
+        for h in range(spread):
+            if residue:
+                by = residue & -residue
+                bases[h][residue] = times(bases[h][residue - by], turns[by])
+            value = bases[h][residue][0]
             if h == 0 and residue == 0:
-                value = jnp.where(lane == half, (1 - 2 * (cd & 1)).astype(F32), u)
+                value = jnp.where(column == half, (1 - 2 * (cd & 1)).astype(F32), value)
             at = (RESIDUES.index(residue) * spread + h) * LANES
             ph[:, at : at + LANES] = value.astype(BF16)
-            if residue < 7:
-                u, v = u * du - v * dv, v * du + u * dv
-
+
+    make_phases(0)
+    make_phases(4)
+    fetches[2].wait()
     lane = iota((16, LANES), 1)
     trial = ((lane // (2 * trials_each)) ^ chan) * trials_each + (lane & (trials_each - 1))
     dm = jnp.concatenate([dm_ref[...], dm_ref[...]], axis=1)
@@ -117,14 +140,8 @@
     imag = (lane & trials_each) != 0
     row = iota((16, LANES), 0)
     own_half = jnp.where(imag, half, 0)
-    edge = jnp.zeros((send_ref.shape[0], EDGE), BF16)
-    for ref in (send_ref, keep_ref):
-        ref[:, :EDGE] = edge
-        ref[:, bins + EDGE :] = edge
-
-    order = class_order()
-    fetch.wait()
     starts = [sum(bins // s for s in STEP[:k]) for k in range(4)]
+    fetches[1].wait()
 
     def turn_tile(t):
         columns = pl.ds(multiple(t * LANES, LANES), LANES)
@@ -137,11 +154,8 @@
                 turned[part, pl.ds(multiple(starts[k] + t * size, 16), size), :] = rows[first : first + size]
                 first += size
 
-    repeat(tiles, turn_tile)
-
     def multiply(k, b, size, y):
-        count = chunks >> k
-        columns = count * LANES
+        columns = (chunks >> k) * LANES
         rows = pl.ds(multiple(starts[k] + b * size, 16), size)
         for part in range(2):
             y[part, :size, :columns] = jnp.dot(
@@ -176,25 +190,6 @@
 
         repeat(size // 16, group)
 
-    size = y0.shape[1]
-    work = [(k, b, min(size, bins // STEP[k])) for k in range(4) for b in range(max(1, bins // STEP[k] // size))]
-    if len(work) <= 16:
-        buffers = (y0, y1)
-        multiply(*work[0], y0)
-        for n, item in enumerate(work):
-            if n + 1 < len(work):
-                multiply(*work[n + 1], buffers[(n + 1) % 2])
-            pick(*item, buffers[n % 2])
-    else:
-        for k in range(4):
-
-            def whole_block(b, carry, k=k):
-                multiply(k, b, min(size, bins // STEP[k]), y0)
-                pick(k, b, min(size, bins // STEP[k]), y0)
-                return carry
-
-            lax.fori_loop(0, max(1, bins // STEP[k] // size), whole_block, 0)
-
     wide = 2 * trials_each
 
     def finish(t):
@@ -205,33 +200,70 @@
             ref = (keep_ref, send_ref)[k % 2]
             ref[(k // 2) * wide : (k // 2 + 1) * wide, columns] = out[k * wide : (k + 1) * wide]
 
-    repeat(tiles, finish)
+    size = y0.shape[1]
+    sizes = [min(size, bins // s) for s in STEP]
+    counts = [bins // s // own for s, own in zip(STEP, sizes)]
+    if tiles <= 8:
+        work = [(k, b, sizes[k]) for k in (3, 2, 1, 0) for b in range(counts[k])]
+        buffers = (y0, y1)
+        for t in range(tiles):
+            turn_tile(t)
+        multiply(*work[0], y0)
+        made = {}
+        for residue in (2, 6, 1, 5, 3, 7):
+            make_phases(residue)
+        per_block = sizes[0] * STEP[0] // LANES
+        for n, item in enumerate(work):
+            for residue in made.get(n, ()):
+                make_phases(residue)
+            if n + 1 < len(work):
+                multiply(*work[n + 1], buffers[(n + 1) % 2])
+            pick(*item, buffers[n % 2])
+            if item[0] == 0:
+                for t in range(item[1] * per_block, (item[1] + 1) * per_block):
+                    finish(t)
+    else:
+        for residue in (2, 6, 1, 5, 3, 7):
+            make_phases(residue)
+        repeat(tiles, turn_tile)
+        for k in range(4):
+
+            def whole_block(b, carry, k=k):
+                multiply(k, b, sizes[k], y0)
+                pick(k, b, sizes[k], y0)
+                return carry
+
+            lax.fori_loop(0, counts[k], whole_block, 0)
+        repeat(tiles, finish)
 
 
 def dedisperse(spectra, dm_trials, chan_delay, trials_each):
     _, channels, bins = spectra.shape
     size = 128
     rows = LANES // 2
+    dm = dm_trials.reshape(1, -1)
     delays = chan_delay.reshape(-1, LANES)
-    shape = jax.ShapeDtypeStruct((rows, bins + 2 * EDGE), BF16)
-    in_vmem = pl.BlockSpec(memory_space=pltpu.VMEM)
+    out = pltpu.VMEM((rows, bins + 2 * EDGE), BF16)
+    room = 12 * rows * (bins + 2 * EDGE) * 2
     return pl.pallas_call(
         functools.partial(dedisperse_kernel, trials_each),
-        in_specs=[in_vmem, in_vmem, pl.BlockSpec(memory_space=pl.ANY)],
-        out_specs=[in_vmem] * 2,
-        out_shape=[shape] * 2,
+        in_specs=[pl.BlockSpec(memory_space=pltpu.HBM)] * 3,
+        out_specs=[pl.BlockSpec(memory_space=pltpu.VMEM)] * 2,
+        out_shape=[out] * 2,
         scratch_shapes=[
+            pltpu.VMEM(dm.shape, jnp.int32),
+            pltpu.VMEM(delays.shape, jnp.int32),
             pltpu.VMEM(spectra.shape, BF16),
             pltpu.VMEM((channels, 2 * bins), BF16),
             pltpu.VMEM((2, bins, channels), BF16),
             pltpu.VMEM((2, size, 2 * bins), BF16),
             pltpu.VMEM((2, size, 2 * bins), BF16),
             pltpu.VMEM((bins, LANES), BF16),
-            pltpu.SemaphoreType.DMA,
+            pltpu.SemaphoreType.DMA((3,)),
         ],
-        compiler_params=pltpu.CompilerParams(vmem_limit_bytes=62 * 2**20),
+        compiler_params=pltpu.CompilerParams(vmem_limit_bytes=min(62 * 2**20, 64 * 2**20 - room)),
         name="dedisperse",
-    )(dm_trials.reshape(1, -1), delays, spectra)
+    )(dm, delays, spectra)
 
 
 def pick_kernel(bank_ref, ids_ref, out_ref):
@@ -258,37 +290,48 @@
     count = template_ids.shape[0]
     return pl.pallas_call(
         pick_kernel,
-        out_shape=jax.ShapeDtypeStruct((2 * count, 2 * taps), BF16),
+        out_shape=pltpu.VMEM((2 * count, 2 * taps), BF16),
         cost_estimate=pl.CostEstimate(flops=4 * count * bank * taps, bytes_accessed=2**20, transcendentals=0),
         name="pick_templates",
     )(template_bank, template_ids.reshape(1, -1))
 
 
-def search_kernel(scale, taps, near_ref, far_ref, templates_ref, out_ref, signal, hankel):
-    step = pl.program_id(0)
-    each, count, bins = out_ref.shape
-    rows, width = near_ref.shape
-    trials = rows // 2
-
-    @pl.when(step == 0)
-    def _():
-        total = near_ref[...].astype(F32) + far_ref[...].astype(F32)
-        signal[...] = (total * scale).astype(BF16).astype(F32)
-
-    for k in range(each):
-        trial = step * each + k
+def search_kernel(scale, near_ref, far_ref, templates_ref, out_hbm, signal, hankel, out, sems):
+    trials, count, bins = out.shape
+    width = near_ref.shape[1]
+    taps = templates_ref.shape[1] // 2
+    total = near_ref[...].astype(F32) + far_ref[...].astype(F32)
+    signal[...] = (total * scale).astype(BF16).astype(F32)
+    each = trials // sems.shape[0]
+    ahead = iota((16, LANES), 1) + 15 - iota((16, LANES), 0)
+    ats = [(ahead + 16 * e & (LANES - 1)).astype(jnp.int16) for e in range(LANES // 16)]
+    stays = [(ahead + 16 * e).astype(jnp.int16) < LANES for e in range(LANES // 16)]
+
+    def fill(trial, to):
         for part in range(2):
             line = signal[pl.ds(part * trials + trial, 1), :]
-            skew = pltpu.roll(jnp.broadcast_to(line, (16, width)), width - 15, 1, stride=1, stride_axis=0)
+            line = jnp.broadcast_to(line, (16, width)).astype(BF16)
+            pieces = [line[:, v * LANES : (v + 1) * LANES] for v in range(width // LANES)]
             for e in range(LANES // 16):
-                moved = skew if e == 0 else pltpu.roll(skew, width - 16 * e, 1)
-                moved = moved.astype(BF16)
+                turned = [lane_gather(piece, ats[e]) for piece in pieces]
+                moved = [jnp.where(stays[e], turned[v], turned[v + 1]) for v in range(len(turned) - 1)]
                 for h in range(taps // LANES):
                     at = part * taps + h * LANES + 16 * e
-                    hankel[k, at : at + 16, :] = moved[:, h * LANES : h * LANES + bins]
-        response = jnp.dot(templates_ref[...], hankel[k], preferred_element_type=F32)
+                    for v in range(bins // LANES):
+                        to[at : at + 16, v * LANES : (v + 1) * LANES] = moved[h + v]
+
+    copies = []
+    for trial in range(trials):
+        fill(trial, hankel.at[trial % 2])
+        response = jnp.dot(templates_ref[...], hankel[trial % 2], preferred_element_type=F32)
         re, im = response[:count], response[count:]
-        out_ref[k] = (re * re + im * im).astype(BF16)
+        out[trial] = (re * re + im * im).astype(BF16)
+        if trial % each == each - 1:
+            here = pl.ds(trial + 1 - each, each)
+            copies.append(pltpu.make_async_copy(out.at[here], out_hbm.at[here], sems.at[trial // each]))
+            copies[-1].start()
+    for copy in copies:
+        copy.wait()
 
 
 def search(near, far, templates, scale, bins):
@@ -296,16 +339,19 @@
     trials = rows // 2
     taps = templates.shape[1] // 2
     count = templates.shape[0] // 2
-    each = min(trials, 4)
-    whole = lambda shape: pl.BlockSpec(shape, lambda i: (0,) * len(shape))
+    in_vmem = pl.BlockSpec(memory_space=pltpu.VMEM)
     return pl.pallas_call(
-        functools.partial(search_kernel, scale, taps),
-        grid=(trials // each,),
-        in_specs=[whole(near.shape), whole(far.shape), whole(templates.shape)],
-        out_specs=pl.BlockSpec((each, count, bins), lambda i: (i, 0, 0)),
+        functools.partial(search_kernel, scale),
+        in_specs=[in_vmem] * 3,
+        out_specs=pl.BlockSpec(memory_space=pltpu.HBM),
         out_shape=jax.ShapeDtypeStruct((trials, count, bins), BF16),
-        scratch_shapes=[pltpu.VMEM((rows, width), F32), pltpu.VMEM((each, 2 * taps, bins), BF16)],
-        compiler_params=pltpu.CompilerParams(vmem_limit_bytes=48 * 2**20),
+        scratch_shapes=[
+            pltpu.VMEM((rows, width), F32),
+            pltpu.VMEM((2, 2 * taps, bins), BF16),
+            pltpu.VMEM((trials, count, bins), BF16),
+            pltpu.SemaphoreType.DMA((min(trials, 4),)),
+        ],
+        compiler_params=pltpu.CompilerParams(vmem_limit_bytes=32 * 2**20),
         name="search",
     )(near, far, templates)
 

time: 29.7 us -> 26 us (0.88)
  Pallas kernels: 12.8 us -> 10.5 us
  local copies, waits for them, and re-layouts: 0.96 us -> 0.01 us
  other arithmetic: 1.03 us -> 0.1 us
  waiting for transfers between devices: 6.48 us -> 6.96 us
    pallas_call x2, Pallas kernels: 6.26 us -> 4.71 us  [the longest x1 3.4 us: search(): pl.pallas_call(functools.partial(search_kernel, scale), in_specs=[in_vmem...]
    unnamed x2 -> x0, local copies, waits for them, and re-layouts: 0.95 us -> none
    convert_element_type x1, other arithmetic: 0.96 us -> 0.04 us  [local(): (keep.astype(F32) + got.astype(F32)).astype(BF16)]
    pallas_call x1, Pallas kernels: 6.56 us -> 5.83 us  [dedisperse(): pl.pallas_call(functools.partial(dedisperse_kernel, trials_each), in_spec...]
    ppermute x4, waiting for transfers between devices: 6.48 us -> 6.96 us  [swap(): lax.ppermute(cells, axis, [(i, i ^ distance) for i in range(lax.axis_size...]
  transfers between devices with their start and end apart: 4 -> 4, of which waited for: 4 -> 4; matrix products, arithmetic and copies ran while one was open for 0% -> 0% of each run, Pallas kernels for 7% -> 5%
where the time goes in v3:
time: 26 us; the launch traced here: 25.8 us
  Pallas kernels  10.5 us (40%)
  starting transfers between devices  8.1 us (31%)
  waiting for transfers between devices  6.96 us (27%)
    ppermute x4, starting transfers between devices, swap(): lax.ppermute(cells, axis, [(i, i ^ distance) for i in range(lax.axis_size...  8.1 us
    ppermute x4, waiting for transfers between devices, swap(): lax.ppermute(cells, axis, [(i, i ^ distance) for i in range(lax.axis_size...  6.96 us
    pallas_call x1, Pallas kernels, dedisperse(): pl.pallas_call(functools.partial(dedisperse_kernel, trials_each), in_spec...  5.83 us
    pallas_call x1, Pallas kernels, search(): pl.pallas_call(functools.partial(search_kernel, scale), in_specs=[in_vmem...  3.4 us
    pallas_call x1, Pallas kernels, pick_templates(): pl.pallas_call(pick_kernel, out_shape=pltpu.VMEM((2 * count, 2 * taps), B...  1.31 us
  transfers between devices with their start and end apart: 4, of which 4 were waited for; matrix products, arithmetic and copies ran while one was open for 0% of the time, Pallas kernels for 5%

profile of v3, /device:TPU:0, one launch (start us, length us, event | category | flops | bytes accessed | tf_op | source)
XLA Modules:
  0.0 25.8 jit_solution(6529488497863624558)
XLA Ops:
  0.0 5.8 %dedisperse.1 = (bf16[64,1280]{1,0:T(8,128)(2,1)S(1)}, bf16[64,1280]{1,0:T(8,128)(2,1)S(1)}) custom-call(s32[1,64]{1,0:T(1,128)} %bitcast.14, s32[32,128]{1,0:T(8,128)} %bitcast.13, bf16[2,256,1024]{2,1,0:T(8,128)(2,1)} %sp_hbm.1), custom_call_target="tpu_custom_call" | custom-call | tf_op jit(solution)/shard_map/dedisperse/pallas_call | solution.py:248
  5.8 0.5 %collective-permute-start = (bf16[64,1280]{1,0:T(8,128)(2,1)S(1)}, bf16[64,1280]{1,0:T(8,128)(2,1)S(1)}, u32[]{:S(2)}, u32[]{:S(2)}) collective-permute-start(bf16[64,1280]{1,0:T(8,128)(2,1)S(1)} %get-tuple-element.8), channel_id=1, source_target_pairs={{0,1},{1,0},{2,3},{3,2},{4,5},{5,4},{6,7},{7,6},{8,9},{9,8},{10,11... | collective-permute-start | bytes 491528 | tf_op jit(solution)/shard_map/ppermute | solution.py:360
  6.4 1.0 %collective-permute-done = bf16[64,1280]{1,0:T(8,128)(2,1)S(1)} collective-permute-done((bf16[64,1280]{1,0:T(8,128)(2,1)S(1)}, bf16[64,1280]{1,0:T(8,128)(2,1)S(1)}, u32[]{:S(2)}, u32[]{:S(2)}) %collective-permute-start) | collective-permute-done | bytes 163872 | tf_op jit(solution)/shard_map/ppermute | solution.py:360
  7.5 2.9 %collective-permute-start.1 = (bf16[32,1280]{1,0:T(8,128)(2,1)S(1)}, bf16[32,1280]{1,0:T(8,128)(2,1)S(1)}, u32[]{:S(2)}, u32[]{:S(2)}) collective-permute-start(bf16[32,1280]{1,0:T(8,128)(2,1)S(1)} %slice_bitcast_fusion), channel_id=1, source_target_pairs={{0,2},{1,3},{2,0},{3,1},{4,6},{5,7},{6,4},{7,5},{8,10},{9,11},{10,... | collective-permute-start | bytes 245768 | tf_op jit(solution)/shard_map/ppermute | solution.py:360
  10.4 2.8 %collective-permute-done.1 = bf16[32,1280]{1,0:T(8,128)(2,1)S(1)} collective-permute-done((bf16[32,1280]{1,0:T(8,128)(2,1)S(1)}, bf16[32,1280]{1,0:T(8,128)(2,1)S(1)}, u32[]{:S(2)}, u32[]{:S(2)}) %collective-permute-start.1) | collective-permute-done | bytes 81952 | tf_op jit(solution)/shard_map/ppermute | solution.py:360
  13.2 2.9 %collective-permute-start.2 = (bf16[32,768]{1,0:T(8,128)(2,1)S(1)}, bf16[32,768]{1,0:T(8,128)(2,1)S(1)}, u32[]{:S(2)}, u32[]{:S(2)}) collective-permute-start(bf16[32,768]{1,0:T(8,128)(2,1)S(1)} %broadcast_select_fusion), channel_id=1, source_target_pairs={{0,8},{4,12},{8,0},{12,4},{1,9},{5,13},{9,1},{13,5},{2,10},{6,14},... | collective-permute-start | bytes 147464 | tf_op jit(solution)/shard_map/ppermute | solution.py:360
  16.1 2.3 %collective-permute-done.2 = bf16[32,768]{1,0:T(8,128)(2,1)S(1)} collective-permute-done((bf16[32,768]{1,0:T(8,128)(2,1)S(1)}, bf16[32,768]{1,0:T(8,128)(2,1)S(1)}, u32[]{:S(2)}, u32[]{:S(2)}) %collective-permute-start.2) | collective-permute-done | bytes 49184 | tf_op jit(solution)/shard_map/ppermute | solution.py:360
  18.4 1.8 %collective-permute-start.3 = (bf16[32,512]{1,0:T(8,128)(2,1)S(1)}, bf16[32,512]{1,0:T(8,128)(2,1)S(1)}, u32[]{:S(2)}, u32[]{:S(2)}) collective-permute-start(bf16[32,512]{1,0:T(8,128)(2,1)S(1)} %get-tuple-element.9), channel_id=1, source_target_pairs={{0,4},{4,0},{8,12},{12,8},{1,5},{5,1},{9,13},{13,9},{2,6},{6,2},{1... | collective-permute-start | bytes 98312 | tf_op jit(solution)/shard_map/ppermute | solution.py:360
  20.1 1.3 %pick_templates.1.templates_ref = bf16[256,512]{1,0:T(8,128)(2,1)S(1)} custom-call(bf16[2,256,256]{2,1,0:T(8,128)(2,1)} %bank_ref.1, s32[1,128]{1,0:T(1,128)} %bitcast.15), custom_call_target="tpu_custom_call" | custom-call | flops 33554432 | bytes 1048576 | tf_op jit(solution)/shard_map/pick_templates/pallas_call | solution.py:291
  21.5 0.9 %collective-permute-done.3.far_ref = bf16[32,512]{1,0:T(8,128)(2,1)S(1)} collective-permute-done((bf16[32,512]{1,0:T(8,128)(2,1)S(1)}, bf16[32,512]{1,0:T(8,128)(2,1)S(1)}, u32[]{:S(2)}, u32[]{:S(2)}) %collective-permute-start.3) | collective-permute-done | bytes 32800 | tf_op jit(solution)/shard_map/ppermute | solution.py:360
  22.4 3.4 %search.1 = bf16[16,128,256]{2,1,0:T(8,128)(2,1)} custom-call(bf16[32,512]{1,0:T(8,128)(2,1)S(1)} %get-tuple-element.10.near_ref, bf16[32,512]{1,0:T(8,128)(2,1)S(1)} %collective-permute-done.3.far_ref, bf16[256,512]{1,0:T(8,128)(2,1)S(1)} %pick_templates.1.templates_ref), custom_call_target="tpu_custom_call" | custom-call | tf_op jit(solution)/shard_map/search/pallas_call | solution.py:343
  (6 shorter events, 0.1 us)
Async XLA Ops:
  5.8 1.6 %collective-permute-start = (bf16[64,1280]{1,0:T(8,128)(2,1)S(1)}, bf16[64,1280]{1,0:T(8,128)(2,1)S(1)}, u32[]{:S(2)}, u32[]{:S(2)}) collective-permute-start(bf16[64,1280]{1,0:T(8,128)(2,1)S(1)} %get-tuple-element.8), channel_id=1, source_target_pairs={{0,1},{1,0},{2,3},{3,2},{4,5},{5,4},{6,7},{7,6},{8,9},{9,8},{10,11... | collective-permute-start | bytes 491528 | tf_op jit(solution)/shard_map/ppermute | solution.py:360
  7.5 5.7 %collective-permute-start.1 = (bf16[32,1280]{1,0:T(8,128)(2,1)S(1)}, bf16[32,1280]{1,0:T(8,128)(2,1)S(1)}, u32[]{:S(2)}, u32[]{:S(2)}) collective-permute-start(bf16[32,1280]{1,0:T(8,128)(2,1)S(1)} %slice_bitcast_fusion), channel_id=1, source_target_pairs={{0,2},{1,3},{2,0},{3,1},{4,6},{5,7},{6,4},{7,5},{8,10},{9,11},{10,... | collective-permute-start | bytes 245768 | tf_op jit(solution)/shard_map/ppermute | solution.py:360
  13.2 5.2 %collective-permute-start.2 = (bf16[32,768]{1,0:T(8,128)(2,1)S(1)}, bf16[32,768]{1,0:T(8,128)(2,1)S(1)}, u32[]{:S(2)}, u32[]{:S(2)}) collective-permute-start(bf16[32,768]{1,0:T(8,128)(2,1)S(1)} %broadcast_select_fusion), channel_id=1, source_target_pairs={{0,8},{4,12},{8,0},{12,4},{1,9},{5,13},{9,1},{13,5},{2,10},{6,14},... | collective-permute-start | bytes 147464 | tf_op jit(solution)/shard_map/ppermute | solution.py:360
  18.4 4.0 %collective-permute-start.3 = (bf16[32,512]{1,0:T(8,128)(2,1)S(1)}, bf16[32,512]{1,0:T(8,128)(2,1)S(1)}, u32[]{:S(2)}, u32[]{:S(2)}) collective-permute-start(bf16[32,512]{1,0:T(8,128)(2,1)S(1)} %get-tuple-element.9), channel_id=1, source_target_pairs={{0,4},{4,0},{8,12},{12,8},{1,5},{5,1},{9,13},{13,9},{2,6},{6,2},{1... | collective-permute-start | bytes 98312 | tf_op jit(solution)/shard_map/ppermute | solution.py:360

commit v4 on v3

--- a/solution.py
+++ b/solution.py
@@ -74,6 +74,12 @@
         bin_of = jnp.where(row >= first, step * (row - first) + start, bin_of)
         first += LANES // step
     return jnp.where(bin_of == column, 1.0, 0.0).astype(BF16)
+
+
+def quarter_turns(value, count):
+    odd = (count & 1) == 1
+    cos, sin = jnp.where(odd, value[1], value[0]), jnp.where(odd, value[0], value[1])
+    return jnp.where(((count + 1) & 2) == 2, -cos, cos), jnp.where((count & 2) == 2, -sin, sin)
 
 
 def times(one, other):
@@ -117,7 +123,12 @@
     turns = {1: sincos(cd & (samples - 1), samples)}
     turns[2] = times(turns[1], turns[1])
     turns[4] = times(turns[2], turns[2])
-    bases = [{0: sincos((start + 8 * half * h * cd) & (samples - 1), samples)} for h in range(spread)]
+    bases = [{0: sincos(start & (samples - 1), samples)}]
+    for h in range(1, spread):
+        if 8 * half * h * 4 == samples:
+            bases.append({0: quarter_turns(bases[0][0], cd)})
+        else:
+            bases.append({0: sincos((start + 8 * half * h * cd) & (samples - 1), samples)})
 
     def make_phases(residue):
         for h in range(spread):
@@ -137,9 +148,12 @@
     trial = ((lane // (2 * trials_each)) ^ chan) * trials_each + (lane & (trials_each - 1))
     dm = jnp.concatenate([dm_ref[...], dm_ref[...]], axis=1)
     dm = jnp.take_along_axis(jnp.broadcast_to(dm, (16, LANES)), trial, axis=1)
-    imag = (lane & trials_each) != 0
+    imag = (lane & trials_each).astype(jnp.int16) != 0
     row = iota((16, LANES), 0)
-    own_half = jnp.where(imag, half, 0)
+    own_half = jnp.where((lane & trials_each) != 0, half, 0).astype(jnp.int16)
+    other_half = own_half ^ half
+    zero, one = jnp.zeros((16, LANES), BF16), jnp.ones((16, LANES), BF16)
+    running = {}
     starts = [sum(bins // s for s in STEP[:k]) for k in range(4)]
     fetches[1].wait()
 
@@ -158,22 +172,29 @@
         columns = (chunks >> k) * LANES
         rows = pl.ds(multiple(starts[k] + b * size, 16), size)
         for part in range(2):
-            y[part, :size, :columns] = jnp.dot(
-                turned[part, rows, :], ph[:, :columns], preferred_element_type=F32
-            ).astype(BF16)
+            for at in range(0, columns, 256):
+                y[part, :size, at : at + 256] = jnp.dot(
+                    turned[part, rows, :], ph[:, at : at + 256], preferred_element_type=F32
+                ).astype(BF16)
 
     def pick(k, b, size, y):
         each = LANES // STEP[k]
         tile_first = sum(LANES // s for s in STEP[:k])
 
-        def group(i):
+        begin = ((STEP[k] * row + FIRST[k]) * dm).astype(jnp.int16)
+        more = (16 * STEP[k] * dm).astype(jnp.int16)
+
+        def group(i, product=None):
             base = b * size + i * 16
-            signed = ((STEP[k] * (base + row) + FIRST[k]) * dm + bins & (samples - 1)) - bins
+            if product is None:
+                product = ((STEP[k] * (base + row) + FIRST[k]) * dm).astype(jnp.int16)
+            unused = 16 - samples.bit_length() + 1
+            signed = lax.shift_left(product, jnp.full_like(product, unused))
+            signed = lax.shift_right_arithmetic(signed, jnp.full_like(signed, unused))
             near = jnp.abs(signed)
-            key = (near & (bins - 1 - 8 * (half - 1))).astype(jnp.int16)
-            at_re = (shift(near, 3) & (half - 1)) ^ own_half ^ jnp.where(signed == -bins, half, 0)
-            at_im = (at_re ^ half).astype(jnp.int16)
-            at_re = at_re.astype(jnp.int16)
+            key = near & (bins - 1 - 8 * (half - 1))
+            at_re = (shift(near, 3) & (half - 1)) ^ jnp.where(signed == -bins, other_half, own_half)
+            at_im = at_re ^ half
             got = []
             for part, at in ((0, at_re), (1, at_im)):
                 value = None
@@ -182,12 +203,21 @@
                     new = lane_gather(y[part, pl.ds(multiple(i * 16, 16), 16), lanes], at)
                     this = RESIDUES[j // spread] + 8 * half * (j % spread)
                     value = new if value is None else jnp.where(key == this, new, value)
-                got.append(value.astype(F32))
-            sign = jnp.where((signed & (bins - 1)) == 0, 0.0, jnp.where(signed < 0, -1.0, 1.0))
-            total = got[0] * jnp.where(imag, -sign, 1.0) + got[1] * jnp.where(imag, 1.0, sign)
+                got.append(value)
+            sign = jnp.where(signed < 0, -one, one)
+            sign = jnp.where((signed & (bins - 1)) == 0, zero, sign)
+            total = got[0] * jnp.where(imag, -sign, one) + got[1] * jnp.where(imag, one, sign)
             at = (base // each) * LANES + tile_first + base % each
-            xs[pl.ds(multiple(at, 16), 16), :] = total.astype(BF16)
-
+            xs[pl.ds(multiple(at, 16), 16), :] = total
+            return product
+
+        if isinstance(b, int) and size // 16 <= 8:
+            product = running.get(k, begin)
+            for i in range(size // 16):
+                group(i, product)
+                product = product + more
+            running[k] = product
+            return
         repeat(size // 16, group)
 
     wide = 2 * trials_each
@@ -356,8 +386,14 @@
     )(near, far, templates)
 
 
-def swap(cells, axis, distance):
-    return lax.ppermute(cells, axis, [(i, i ^ distance) for i in range(lax.axis_size(axis))])
+def swap(cells, owner_bit, span_bit):
+    owners, spans = lax.axis_size("chan"), lax.axis_size("bin")
+    pairs = [(i, i ^ (span_bit * owners + owner_bit)) for i in range(owners * spans)]
+    return lax.ppermute(cells, ("bin", "chan"), pairs)
+
+
+def add(*cells):
+    return sum(cell.astype(F32) for cell in cells).astype(BF16)
 
 
 def local(spectra, dm_trials, chan_delay, template_bank, template_ids):
@@ -367,26 +403,35 @@
     trials_each = dm_trials.shape[0] // owners
     scale = 1.0 / math.sqrt(chan_delay.shape[0])
     wide = 2 * trials_each
+    place = lax.axis_index("bin")
     templates = pick_templates(template_bank, template_ids)
     send, keep = dedisperse(spectra, dm_trials, chan_delay, trials_each)
     distance = 1
+    while 2 * distance < owners:
+        total = add(keep, swap(send, distance, 0)).reshape(-1, 2, wide, keep.shape[1])
+        keep, send = total[:, 0].reshape(-1, keep.shape[1]), total[:, 1].reshape(-1, keep.shape[1])
+        distance *= 2
+    reach = (spans - 1) * own_bins + 2 * EDGE
+    odd = (place & 1) != 0
+
+    def by_parity(cells):
+        low, high = cells[:, :reach], cells[:, own_bins : own_bins + reach]
+        return jnp.where(odd, high, low), jnp.where(odd, low, high)
+
+    keep, keep_far = by_parity(keep)
+    send, send_far = by_parity(send)
+    keep = add(keep, swap(send, distance, 0), swap(keep_far, 0, 1), swap(send_far, distance, 1))
+    part = spans // 2
     while True:
-        got = swap(send, "chan", distance)
-        distance *= 2
-        if distance == owners:
-            break
-        total = (keep.astype(F32) + got.astype(F32)).astype(BF16).reshape(-1, 2, wide, keep.shape[1])
-        keep, send = total[:, 0].reshape(-1, keep.shape[1]), total[:, 1].reshape(-1, keep.shape[1])
-    place = lax.axis_index("bin")
-    part = spans // 2
-    while part:
-        total = (keep.astype(F32) + got.astype(F32)).astype(BF16)
-        left, right = total[:, : part * own_bins + 2 * EDGE], total[:, part * own_bins :]
+        width = (part // 2 - 1) * 2 * own_bins + own_bins + 2 * EDGE
         upper = (place & part) != 0
+        left, right = keep[:, :width], keep[:, part * own_bins : part * own_bins + width]
         keep, send = jnp.where(upper, right, left), jnp.where(upper, left, right)
-        got = swap(send, "bin", part)
+        got = swap(send, 0, part)
+        if part == 2:
+            return search(keep, got, templates, scale, own_bins)
+        keep = add(keep, got)
         part //= 2
-    return search(keep, got, templates, scale, own_bins)
 
 
 def solution(mesh):

time: 26 us -> 25.5 us (0.981)
  Pallas kernels: 10.5 us -> 10 us
  starting transfers between devices: 8.1 us -> 7.73 us
  waiting for transfers between devices: 6.96 us -> 7.27 us
    pallas_call x1, Pallas kernels: 5.83 us -> 5.32 us  [dedisperse(): pl.pallas_call(functools.partial(dedisperse_kernel, trials_each), in_spec...]
    ppermute x4 -> x5, starting transfers between devices: 8.1 us -> 7.73 us  [swap(): return lax.ppermute(cells, ('bin', 'chan'), pairs)]
    ppermute x4 -> x5, waiting for transfers between devices: 6.96 us -> 7.27 us  [swap(): return lax.ppermute(cells, ('bin', 'chan'), pairs)]
  transfers between devices with their start and end apart: 4 -> 5, of which waited for: 4 -> 5; matrix products, arithmetic and copies ran while one was open for 0% -> 0% of each run, Pallas kernels for 5% -> 5%
where the time goes in v4:
time: 25.5 us; the launch traced here: 25.2 us
  Pallas kernels  10 us (39%)
  starting transfers between devices  7.73 us (30%)
  waiting for transfers between devices  7.27 us (29%)
    ppermute x5, starting transfers between devices, swap(): return lax.ppermute(cells, ('bin', 'chan'), pairs)  7.73 us
    ppermute x5, waiting for transfers between devices, swap(): return lax.ppermute(cells, ('bin', 'chan'), pairs)  7.27 us
    pallas_call x1, Pallas kernels, dedisperse(): pl.pallas_call(functools.partial(dedisperse_kernel, trials_each), in_spec...  5.32 us
    pallas_call x1, Pallas kernels, search(): pl.pallas_call(functools.partial(search_kernel, scale), in_specs=[in_vmem...  3.4 us
    pallas_call x1, Pallas kernels, pick_templates(): pl.pallas_call(pick_kernel, out_shape=pltpu.VMEM((2 * count, 2 * taps), B...  1.31 us
  transfers between devices with their start and end apart: 5, of which 5 were waited for; matrix products, arithmetic and copies ran while one was open for 0% of the time, Pallas kernels for 5%

profile of v4, /device:TPU:0, one launch (start us, length us, event | category | flops | bytes accessed | tf_op | source)
XLA Modules:
  0.0 25.2 jit_solution(797778949517315581)
XLA Ops:
  0.0 5.3 %dedisperse.1 = (bf16[64,1280]{1,0:T(8,128)(2,1)S(1)}, bf16[64,1280]{1,0:T(8,128)(2,1)S(1)}) custom-call(s32[1,64]{1,0:T(1,128)} %bitcast.10, s32[32,128]{1,0:T(8,128)} %bitcast.9, bf16[2,256,1024]{2,1,0:T(8,128)(2,1)} %sp_hbm.1), custom_call_target="tpu_custom_call" | custom-call | tf_op jit(solution)/shard_map/dedisperse/pallas_call | solution.py:278
  5.3 0.5 %collective-permute-start = (bf16[64,1280]{1,0:T(8,128)(2,1)S(1)}, bf16[64,1280]{1,0:T(8,128)(2,1)S(1)}, u32[]{:S(2)}, u32[]{:S(2)}) collective-permute-start(bf16[64,1280]{1,0:T(8,128)(2,1)S(1)} %get-tuple-element.8), channel_id=1, source_target_pairs={{0,1},{1,0},{2,3},{3,2},{4,5},{5,4},{6,7},{7,6},{8,9},{9,8},{10,11... | collective-permute-start | bytes 491528 | tf_op jit(solution)/shard_map/ppermute | solution.py:392
  5.8 1.0 %collective-permute-done = bf16[64,1280]{1,0:T(8,128)(2,1)S(1)} collective-permute-done((bf16[64,1280]{1,0:T(8,128)(2,1)S(1)}, bf16[64,1280]{1,0:T(8,128)(2,1)S(1)}, u32[]{:S(2)}, u32[]{:S(2)}) %collective-permute-start) | collective-permute-done | bytes 163872 | tf_op jit(solution)/shard_map/ppermute | solution.py:392
  7.0 3.0 %collective-permute-start.2 = (bf16[32,1024]{1,0:T(8,128)(2,1)S(1)}, bf16[32,1024]{1,0:T(8,128)(2,1)S(1)}, u32[]{:S(2)}, u32[]{:S(2)}) collective-permute-start(bf16[32,1024]{1,0:T(8,128)(2,1)S(1)} %broadcast_select_fusion.1), channel_id=1, source_target_pairs={{0,4},{1,5},{2,6},{3,7},{4,0},{5,1},{6,2},{7,3},{8,12},{9,13},{10,... | collective-permute-start | bytes 196616 | tf_op jit(solution)/shard_map/ppermute | solution.py:392
  10.0 1.5 %collective-permute-start.1 = (bf16[32,1024]{1,0:T(8,128)(2,1)S(1)}, bf16[32,1024]{1,0:T(8,128)(2,1)S(1)}, u32[]{:S(2)}, u32[]{:S(2)}) collective-permute-start(bf16[32,1024]{1,0:T(8,128)(2,1)S(1)} %get-tuple-element.11), channel_id=1, source_target_pairs={{0,2},{1,3},{2,0},{3,1},{4,6},{5,7},{6,4},{7,5},{8,10},{9,11},{10,... | collective-permute-start | bytes 196616 | tf_op jit(solution)/shard_map/ppermute | solution.py:392
  11.5 0.1 collective-permute-start.3
  11.5 0.9 %collective-permute-done.2 = bf16[32,1024]{1,0:T(8,128)(2,1)S(1)} collective-permute-done((bf16[32,1024]{1,0:T(8,128)(2,1)S(1)}, bf16[32,1024]{1,0:T(8,128)(2,1)S(1)}, u32[]{:S(2)}, u32[]{:S(2)}) %collective-permute-start.2) | collective-permute-done | bytes 65568 | tf_op jit(solution)/shard_map/ppermute | solution.py:392
  12.4 1.9 %collective-permute-done.1 = bf16[32,1024]{1,0:T(8,128)(2,1)S(1)} collective-permute-done((bf16[32,1024]{1,0:T(8,128)(2,1)S(1)}, bf16[32,1024]{1,0:T(8,128)(2,1)S(1)}, u32[]{:S(2)}, u32[]{:S(2)}) %collective-permute-start.1) | collective-permute-done | bytes 65568 | tf_op jit(solution)/shard_map/ppermute | solution.py:392
  14.3 2.4 %collective-permute-done.3 = bf16[32,1024]{1,0:T(8,128)(2,1)S(1)} collective-permute-done((bf16[32,1024]{1,0:T(8,128)(2,1)S(1)}, bf16[32,1024]{1,0:T(8,128)(2,1)S(1)}, u32[]{:S(2)}, u32[]{:S(2)}) %collective-permute-start.3) | collective-permute-done | bytes 65568 | tf_op jit(solution)/shard_map/ppermute | solution.py:392
  16.7 2.7 %collective-permute-start.4 = (bf16[32,512]{1,0:T(8,128)(2,1)S(1)}, bf16[32,512]{1,0:T(8,128)(2,1)S(1)}, u32[]{:S(2)}, u32[]{:S(2)}) collective-permute-start(bf16[32,512]{1,0:T(8,128)(2,1)S(1)} %get-tuple-element.13), channel_id=1, source_target_pairs={{0,8},{1,9},{2,10},{3,11},{4,12},{5,13},{6,14},{7,15},{8,0},{9,1},... | collective-permute-start | bytes 98312 | tf_op jit(solution)/shard_map/ppermute | solution.py:392
  19.4 1.3 %pick_templates.1.templates_ref = bf16[256,512]{1,0:T(8,128)(2,1)S(1)} custom-call(bf16[2,256,256]{2,1,0:T(8,128)(2,1)} %bank_ref.1, s32[1,128]{1,0:T(1,128)} %bitcast.11), custom_call_target="tpu_custom_call" | custom-call | flops 33554432 | bytes 1048576 | tf_op jit(solution)/shard_map/pick_templates/pallas_call | solution.py:321
  20.7 1.1 %collective-permute-done.4.far_ref = bf16[32,512]{1,0:T(8,128)(2,1)S(1)} collective-permute-done((bf16[32,512]{1,0:T(8,128)(2,1)S(1)}, bf16[32,512]{1,0:T(8,128)(2,1)S(1)}, u32[]{:S(2)}, u32[]{:S(2)}) %collective-permute-start.4) | collective-permute-done | bytes 32800 | tf_op jit(solution)/shard_map/ppermute | solution.py:392
  21.8 3.4 %search.1 = bf16[16,128,256]{2,1,0:T(8,128)(2,1)} custom-call(bf16[32,512]{1,0:T(8,128)(2,1)S(1)} %get-tuple-element.14.near_ref, bf16[32,512]{1,0:T(8,128)(2,1)S(1)} %collective-permute-done.4.far_ref, bf16[256,512]{1,0:T(8,128)(2,1)S(1)} %pick_templates.1.templates_ref), custom_call_target="tpu_custom_call" | custom-call | tf_op jit(solution)/shard_map/search/pallas_call | solution.py:373
  (6 shorter events, 0.1 us)
Async XLA Ops:
  5.3 1.5 %collective-permute-start = (bf16[64,1280]{1,0:T(8,128)(2,1)S(1)}, bf16[64,1280]{1,0:T(8,128)(2,1)S(1)}, u32[]{:S(2)}, u32[]{:S(2)}) collective-permute-start(bf16[64,1280]{1,0:T(8,128)(2,1)S(1)} %get-tuple-element.8), channel_id=1, source_target_pairs={{0,1},{1,0},{2,3},{3,2},{4,5},{5,4},{6,7},{7,6},{8,9},{9,8},{10,11... | collective-permute-start | bytes 491528 | tf_op jit(solution)/shard_map/ppermute | solution.py:392
  7.0 5.4 %collective-permute-start.2 = (bf16[32,1024]{1,0:T(8,128)(2,1)S(1)}, bf16[32,1024]{1,0:T(8,128)(2,1)S(1)}, u32[]{:S(2)}, u32[]{:S(2)}) collective-permute-start(bf16[32,1024]{1,0:T(8,128)(2,1)S(1)} %broadcast_select_fusion.1), channel_id=1, source_target_pairs={{0,4},{1,5},{2,6},{3,7},{4,0},{5,1},{6,2},{7,3},{8,12},{9,13},{10,... | collective-permute-start | bytes 196616 | tf_op jit(solution)/shard_map/ppermute | solution.py:392
  10.0 4.3 %collective-permute-start.1 = (bf16[32,1024]{1,0:T(8,128)(2,1)S(1)}, bf16[32,1024]{1,0:T(8,128)(2,1)S(1)}, u32[]{:S(2)}, u32[]{:S(2)}) collective-permute-start(bf16[32,1024]{1,0:T(8,128)(2,1)S(1)} %get-tuple-element.11), channel_id=1, source_target_pairs={{0,2},{1,3},{2,0},{3,1},{4,6},{5,7},{6,4},{7,5},{8,10},{9,11},{10,... | collective-permute-start | bytes 196616 | tf_op jit(solution)/shard_map/ppermute | solution.py:392
  11.5 5.2 %collective-permute-start.3 = (bf16[32,1024]{1,0:T(8,128)(2,1)S(1)}, bf16[32,1024]{1,0:T(8,128)(2,1)S(1)}, u32[]{:S(2)}, u32[]{:S(2)}) collective-permute-start(bf16[32,1024]{1,0:T(8,128)(2,1)S(1)} %get-tuple-element.12), channel_id=1, source_target_pairs={{0,6},{1,7},{2,4},{3,5},{4,2},{5,3},{6,0},{7,1},{8,14},{9,15},{10,... | collective-permute-start | bytes 196616 | tf_op jit(solution)/shard_map/ppermute | solution.py:392
  16.7 5.1 %collective-permute-start.4 = (bf16[32,512]{1,0:T(8,128)(2,1)S(1)}, bf16[32,512]{1,0:T(8,128)(2,1)S(1)}, u32[]{:S(2)}, u32[]{:S(2)}) collective-permute-start(bf16[32,512]{1,0:T(8,128)(2,1)S(1)} %get-tuple-element.13), channel_id=1, source_target_pairs={{0,8},{1,9},{2,10},{3,11},{4,12},{5,13},{6,14},{7,15},{8,0},{9,1},... | collective-permute-start | bytes 98312 | tf_op jit(solution)/shard_map/ppermute | solution.py:392

commit v5 on v4

--- a/solution.py
+++ b/solution.py
@@ -326,7 +326,7 @@
     )(template_bank, template_ids.reshape(1, -1))
 
 
-def search_kernel(scale, near_ref, far_ref, templates_ref, out_hbm, signal, hankel, out, sems):
+def search_kernel(scale, near_ref, far_ref, templates_ref, out_hbm, signal, out, sems):
     trials, count, bins = out.shape
     width = near_ref.shape[1]
     taps = templates_ref.shape[1] // 2
@@ -337,23 +337,26 @@
     ats = [(ahead + 16 * e & (LANES - 1)).astype(jnp.int16) for e in range(LANES // 16)]
     stays = [(ahead + 16 * e).astype(jnp.int16) < LANES for e in range(LANES // 16)]
 
-    def fill(trial, to):
-        for part in range(2):
-            line = signal[pl.ds(part * trials + trial, 1), :]
-            line = jnp.broadcast_to(line, (16, width)).astype(BF16)
-            pieces = [line[:, v * LANES : (v + 1) * LANES] for v in range(width // LANES)]
+    def fill(trial, part):
+        line = signal[pl.ds(part * trials + trial, 1), :]
+        line = jnp.broadcast_to(line, (16, width)).astype(BF16)
+        pieces = [line[:, v * LANES : (v + 1) * LANES] for v in range(width // LANES)]
+        moved = []
+        for e in range(LANES // 16):
+            turned = [lane_gather(piece, ats[e]) for piece in pieces]
+            moved.append([jnp.where(stays[e], turned[v], turned[v + 1]) for v in range(len(turned) - 1)])
+        rows = []
+        for h in range(taps // LANES):
             for e in range(LANES // 16):
-                turned = [lane_gather(piece, ats[e]) for piece in pieces]
-                moved = [jnp.where(stays[e], turned[v], turned[v + 1]) for v in range(len(turned) - 1)]
-                for h in range(taps // LANES):
-                    at = part * taps + h * LANES + 16 * e
-                    for v in range(bins // LANES):
-                        to[at : at + 16, v * LANES : (v + 1) * LANES] = moved[h + v]
+                rows.append(jnp.concatenate([moved[e][h + v] for v in range(bins // LANES)], axis=1))
+        return jnp.concatenate(rows, axis=0)
 
     copies = []
     for trial in range(trials):
-        fill(trial, hankel.at[trial % 2])
-        response = jnp.dot(templates_ref[...], hankel[trial % 2], preferred_element_type=F32)
+        response = sum(
+            jnp.dot(templates_ref[:, part * taps : (part + 1) * taps], fill(trial, part), preferred_element_type=F32)
+            for part in range(2)
+        )
         re, im = response[:count], response[count:]
         out[trial] = (re * re + im * im).astype(BF16)
         if trial % each == each - 1:
@@ -377,7 +380,6 @@
         out_shape=jax.ShapeDtypeStruct((trials, count, bins), BF16),
         scratch_shapes=[
             pltpu.VMEM((rows, width), F32),
-            pltpu.VMEM((2, 2 * taps, bins), BF16),
             pltpu.VMEM((trials, count, bins), BF16),
             pltpu.SemaphoreType.DMA((min(trials, 4),)),
         ],
@@ -420,7 +422,8 @@
 
     keep, keep_far = by_parity(keep)
     send, send_far = by_parity(send)
-    keep = add(keep, swap(send, distance, 0), swap(keep_far, 0, 1), swap(send_far, distance, 1))
+    send_far, keep_far, send = lax.optimization_barrier((send_far, keep_far, send))
+    keep = add(keep, swap(send_far, distance, 1), swap(keep_far, 0, 1), swap(send, distance, 0))
     part = spans // 2
     while True:
         width = (part // 2 - 1) * 2 * own_bins + own_bins + 2 * EDGE

time: 25.5 us -> 23.8 us (0.933)
  waiting for transfers between devices: 7.27 us -> 6 us
  Pallas kernels: 10 us -> 9.66 us
    ppermute x5, waiting for transfers between devices: 7.27 us -> 6 us  [swap(): return lax.ppermute(cells, ('bin', 'chan'), pairs)]
    pallas_call x1, Pallas kernels: 3.4 us -> 3.03 us  [search(): pl.pallas_call(functools.partial(search_kernel, scale), in_specs=[in_vmem...]
  transfers between devices with their start and end apart: 5 -> 5, of which waited for: 5 -> 5; matrix products, arithmetic and copies ran while one was open for 0% -> 0% of each run, Pallas kernels for 5% -> 6%
where the time goes in v5:
time: 23.8 us; the launch traced here: 23.6 us
  Pallas kernels  9.66 us (41%)
  starting transfers between devices  7.75 us (33%)
  waiting for transfers between devices  6 us (25%)
    ppermute x5, starting transfers between devices, swap(): return lax.ppermute(cells, ('bin', 'chan'), pairs)  7.75 us
    ppermute x5, waiting for transfers between devices, swap(): return lax.ppermute(cells, ('bin', 'chan'), pairs)  6 us
    pallas_call x1, Pallas kernels, dedisperse(): pl.pallas_call(functools.partial(dedisperse_kernel, trials_each), in_spec...  5.32 us
    pallas_call x1, Pallas kernels, search(): pl.pallas_call(functools.partial(search_kernel, scale), in_specs=[in_vmem...  3.03 us
    pallas_call x1, Pallas kernels, pick_templates(): pl.pallas_call(pick_kernel, out_shape=pltpu.VMEM((2 * count, 2 * taps), B...  1.31 us
  transfers between devices with their start and end apart: 5, of which 5 were waited for; matrix products, arithmetic and copies ran while one was open for 0% of the time, Pallas kernels for 6%

profile of v5, /device:TPU:0, one launch (start us, length us, event | category | flops | bytes accessed | tf_op | source)
XLA Modules:
  0.0 23.6 jit_solution(14071317591042896803)
XLA Ops:
  0.0 5.3 %dedisperse.1 = (bf16[64,1280]{1,0:T(8,128)(2,1)S(1)}, bf16[64,1280]{1,0:T(8,128)(2,1)S(1)}) custom-call(s32[1,64]{1,0:T(1,128)} %bitcast.10, s32[32,128]{1,0:T(8,128)} %bitcast.9, bf16[2,256,1024]{2,1,0:T(8,128)(2,1)} %sp_hbm.1), custom_call_target="tpu_custom_call" | custom-call | tf_op jit(solution)/shard_map/dedisperse/pallas_call | solution.py:278
  5.3 0.5 %collective-permute-start = (bf16[64,1280]{1,0:T(8,128)(2,1)S(1)}, bf16[64,1280]{1,0:T(8,128)(2,1)S(1)}, u32[]{:S(2)}, u32[]{:S(2)}) collective-permute-start(bf16[64,1280]{1,0:T(8,128)(2,1)S(1)} %get-tuple-element.11), channel_id=1, source_target_pairs={{0,1},{1,0},{2,3},{3,2},{4,5},{5,4},{6,7},{7,6},{8,9},{9,8},{10,11... | collective-permute-start | bytes 491528 | tf_op jit(solution)/shard_map/ppermute | solution.py:394
  5.8 1.0 %collective-permute-done = bf16[64,1280]{1,0:T(8,128)(2,1)S(1)} collective-permute-done((bf16[64,1280]{1,0:T(8,128)(2,1)S(1)}, bf16[64,1280]{1,0:T(8,128)(2,1)S(1)}, u32[]{:S(2)}, u32[]{:S(2)}) %collective-permute-start) | collective-permute-done | bytes 163872 | tf_op jit(solution)/shard_map/ppermute | solution.py:394
  7.0 3.9 %collective-permute-start.1 = (bf16[32,1024]{1,0:T(8,128)(2,1)S(1)}, bf16[32,1024]{1,0:T(8,128)(2,1)S(1)}, u32[]{:S(2)}, u32[]{:S(2)}) collective-permute-start(bf16[32,1024]{1,0:T(8,128)(2,1)S(1)} %get-tuple-element.12), channel_id=1, source_target_pairs={{0,6},{1,7},{2,4},{3,5},{4,2},{5,3},{6,0},{7,1},{8,14},{9,15},{10,... | collective-permute-start | bytes 196616 | tf_op jit(solution)/shard_map/ppermute | solution.py:394
  10.9 0.4 %collective-permute-start.2 = (bf16[32,1024]{1,0:T(8,128)(2,1)S(1)}, bf16[32,1024]{1,0:T(8,128)(2,1)S(1)}, u32[]{:S(2)}, u32[]{:S(2)}) collective-permute-start(bf16[32,1024]{1,0:T(8,128)(2,1)S(1)} %get-tuple-element.13), channel_id=1, source_target_pairs={{0,4},{1,5},{2,6},{3,7},{4,0},{5,1},{6,2},{7,3},{8,12},{9,13},{10,... | collective-permute-start | bytes 196616 | tf_op jit(solution)/shard_map/ppermute | solution.py:394
  11.4 0.2 collective-permute-start.3
  11.5 1.8 %collective-permute-done.1 = bf16[32,1024]{1,0:T(8,128)(2,1)S(1)} collective-permute-done((bf16[32,1024]{1,0:T(8,128)(2,1)S(1)}, bf16[32,1024]{1,0:T(8,128)(2,1)S(1)}, u32[]{:S(2)}, u32[]{:S(2)}) %collective-permute-start.1) | collective-permute-done | bytes 65568 | tf_op jit(solution)/shard_map/ppermute | solution.py:394
  13.3 1.9 %collective-permute-done.2 = bf16[32,1024]{1,0:T(8,128)(2,1)S(1)} collective-permute-done((bf16[32,1024]{1,0:T(8,128)(2,1)S(1)}, bf16[32,1024]{1,0:T(8,128)(2,1)S(1)}, u32[]{:S(2)}, u32[]{:S(2)}) %collective-permute-start.2) | collective-permute-done | bytes 65568 | tf_op jit(solution)/shard_map/ppermute | solution.py:394
  15.2 0.4 %collective-permute-done.3 = bf16[32,1024]{1,0:T(8,128)(2,1)S(1)} collective-permute-done((bf16[32,1024]{1,0:T(8,128)(2,1)S(1)}, bf16[32,1024]{1,0:T(8,128)(2,1)S(1)}, u32[]{:S(2)}, u32[]{:S(2)}) %collective-permute-start.3) | collective-permute-done | bytes 65568 | tf_op jit(solution)/shard_map/ppermute | solution.py:394
  15.7 2.7 %collective-permute-start.4 = (bf16[32,512]{1,0:T(8,128)(2,1)S(1)}, bf16[32,512]{1,0:T(8,128)(2,1)S(1)}, u32[]{:S(2)}, u32[]{:S(2)}) collective-permute-start(bf16[32,512]{1,0:T(8,128)(2,1)S(1)} %get-tuple-element.19), channel_id=1, source_target_pairs={{0,8},{1,9},{2,10},{3,11},{4,12},{5,13},{6,14},{7,15},{8,0},{9,1},... | collective-permute-start | bytes 98312 | tf_op jit(solution)/shard_map/ppermute | solution.py:394
  18.3 1.3 %pick_templates.1.templates_ref = bf16[256,512]{1,0:T(8,128)(2,1)S(1)} custom-call(bf16[2,256,256]{2,1,0:T(8,128)(2,1)} %bank_ref.1, s32[1,128]{1,0:T(1,128)} %bitcast.11), custom_call_target="tpu_custom_call" | custom-call | flops 33554432 | bytes 1048576 | tf_op jit(solution)/shard_map/pick_templates/pallas_call | solution.py:321
  19.7 0.9 %collective-permute-done.4.far_ref = bf16[32,512]{1,0:T(8,128)(2,1)S(1)} collective-permute-done((bf16[32,512]{1,0:T(8,128)(2,1)S(1)}, bf16[32,512]{1,0:T(8,128)(2,1)S(1)}, u32[]{:S(2)}, u32[]{:S(2)}) %collective-permute-start.4) | collective-permute-done | bytes 32800 | tf_op jit(solution)/shard_map/ppermute | solution.py:394
  20.6 3.0 %search.1 = bf16[16,128,256]{2,1,0:T(8,128)(2,1)} custom-call(bf16[32,512]{1,0:T(8,128)(2,1)S(1)} %get-tuple-element.20.near_ref, bf16[32,512]{1,0:T(8,128)(2,1)S(1)} %collective-permute-done.4.far_ref, bf16[256,512]{1,0:T(8,128)(2,1)S(1)} %pick_templates.1.templates_ref), custom_call_target="tpu_custom_call" | custom-call | tf_op jit(solution)/shard_map/search/pallas_call | solution.py:376
  (5 shorter events, 0.1 us)
Async XLA Ops:
  5.3 1.5 %collective-permute-start = (bf16[64,1280]{1,0:T(8,128)(2,1)S(1)}, bf16[64,1280]{1,0:T(8,128)(2,1)S(1)}, u32[]{:S(2)}, u32[]{:S(2)}) collective-permute-start(bf16[64,1280]{1,0:T(8,128)(2,1)S(1)} %get-tuple-element.11), channel_id=1, source_target_pairs={{0,1},{1,0},{2,3},{3,2},{4,5},{5,4},{6,7},{7,6},{8,9},{9,8},{10,11... | collective-permute-start | bytes 491528 | tf_op jit(solution)/shard_map/ppermute | solution.py:394
  7.0 6.3 %collective-permute-start.1 = (bf16[32,1024]{1,0:T(8,128)(2,1)S(1)}, bf16[32,1024]{1,0:T(8,128)(2,1)S(1)}, u32[]{:S(2)}, u32[]{:S(2)}) collective-permute-start(bf16[32,1024]{1,0:T(8,128)(2,1)S(1)} %get-tuple-element.12), channel_id=1, source_target_pairs={{0,6},{1,7},{2,4},{3,5},{4,2},{5,3},{6,0},{7,1},{8,14},{9,15},{10,... | collective-permute-start | bytes 196616 | tf_op jit(solution)/shard_map/ppermute | solution.py:394
  10.9 4.3 %collective-permute-start.2 = (bf16[32,1024]{1,0:T(8,128)(2,1)S(1)}, bf16[32,1024]{1,0:T(8,128)(2,1)S(1)}, u32[]{:S(2)}, u32[]{:S(2)}) collective-permute-start(bf16[32,1024]{1,0:T(8,128)(2,1)S(1)} %get-tuple-element.13), channel_id=1, source_target_pairs={{0,4},{1,5},{2,6},{3,7},{4,0},{5,1},{6,2},{7,3},{8,12},{9,13},{10,... | collective-permute-start | bytes 196616 | tf_op jit(solution)/shard_map/ppermute | solution.py:394
  11.4 4.3 %collective-permute-start.3 = (bf16[32,1024]{1,0:T(8,128)(2,1)S(1)}, bf16[32,1024]{1,0:T(8,128)(2,1)S(1)}, u32[]{:S(2)}, u32[]{:S(2)}) collective-permute-start(bf16[32,1024]{1,0:T(8,128)(2,1)S(1)} %get-tuple-element.14), channel_id=1, source_target_pairs={{0,2},{1,3},{2,0},{3,1},{4,6},{5,7},{6,4},{7,5},{8,10},{9,11},{10,... | collective-permute-start | bytes 196616 | tf_op jit(solution)/shard_map/ppermute | solution.py:394
  15.7 4.9 %collective-permute-start.4 = (bf16[32,512]{1,0:T(8,128)(2,1)S(1)}, bf16[32,512]{1,0:T(8,128)(2,1)S(1)}, u32[]{:S(2)}, u32[]{:S(2)}) collective-permute-start(bf16[32,512]{1,0:T(8,128)(2,1)S(1)} %get-tuple-element.19), channel_id=1, source_target_pairs={{0,8},{1,9},{2,10},{3,11},{4,12},{5,13},{6,14},{7,15},{8,0},{9,1},... | collective-permute-start | bytes 98312 | tf_op jit(solution)/shard_map/ppermute | solution.py:394

commit v6 on v5

--- a/solution.py
+++ b/solution.py
@@ -111,16 +111,20 @@
 
     fetches[0].wait()
     if channels >= LANES:
-        rows = [cd_ref[pl.ds(block * (channels // LANES) + k, 1), :] for k in range(channels // LANES)]
-        cd = jnp.concatenate([jnp.broadcast_to(row, (LANES, LANES)).T for row in rows], axis=0)
+        lines = [cd_ref[pl.ds(block * (channels // LANES) + k, 1), :] for k in range(channels // LANES)]
     else:
         first = block * channels
-        row = cd_ref[pl.ds(first // LANES, 1), :]
-        moved = pltpu.roll(jnp.broadcast_to(row, (LANES, LANES)), (LANES - first % LANES) % LANES, 1)
-        cd = moved.T[:channels]
+        line = cd_ref[pl.ds(first // LANES, 1), :]
+        lines = [pltpu.roll(jnp.broadcast_to(line, (SUB, LANES)), (LANES - first % LANES) % LANES, 1)[:1]]
+
+    def to_column(lines):
+        return jnp.concatenate([jnp.broadcast_to(line, (LANES, LANES)).T for line in lines], axis=0)[:channels]
+
+    cd = to_column(lines)
+    own_turns = [sincos(line & (samples - 1), samples) for line in lines]
     column = iota(cd.shape, 1)
     start = 8 * (column & (half - 1)) * cd - jnp.where(column >= half, samples // 4, 0)
-    turns = {1: sincos(cd & (samples - 1), samples)}
+    turns = {1: tuple(to_column([turn[n] for turn in own_turns]) for n in range(2))}
     turns[2] = times(turns[1], turns[1])
     turns[4] = times(turns[2], turns[2])
     bases = [{0: sincos(start & (samples - 1), samples)}]
@@ -141,8 +145,9 @@
             at = (RESIDUES.index(residue) * spread + h) * LANES
             ph[:, at : at + LANES] = value.astype(BF16)
 
-    make_phases(0)
-    make_phases(4)
+    for residue in (0, 4, 2, 6, 1, 5, 3, 7):
+        make_phases(residue)
+    fetches[1].wait()
     fetches[2].wait()
     lane = iota((16, LANES), 1)
     trial = ((lane // (2 * trials_each)) ^ chan) * trials_each + (lane & (trials_each - 1))
@@ -155,7 +160,6 @@
     zero, one = jnp.zeros((16, LANES), BF16), jnp.ones((16, LANES), BF16)
     running = {}
     starts = [sum(bins // s for s in STEP[:k]) for k in range(4)]
-    fetches[1].wait()
 
     def turn_tile(t):
         columns = pl.ds(multiple(t * LANES, LANES), LANES)
@@ -234,27 +238,18 @@
     sizes = [min(size, bins // s) for s in STEP]
     counts = [bins // s // own for s, own in zip(STEP, sizes)]
     if tiles <= 8:
-        work = [(k, b, sizes[k]) for k in (3, 2, 1, 0) for b in range(counts[k])]
+        work = [(k, b, sizes[k]) for k in (0, 1, 2, 3) for b in range(counts[k])]
         buffers = (y0, y1)
         for t in range(tiles):
             turn_tile(t)
         multiply(*work[0], y0)
-        made = {}
-        for residue in (2, 6, 1, 5, 3, 7):
-            make_phases(residue)
-        per_block = sizes[0] * STEP[0] // LANES
         for n, item in enumerate(work):
-            for residue in made.get(n, ()):
-                make_phases(residue)
             if n + 1 < len(work):
                 multiply(*work[n + 1], buffers[(n + 1) % 2])
             pick(*item, buffers[n % 2])
-            if item[0] == 0:
-                for t in range(item[1] * per_block, (item[1] + 1) * per_block):
-                    finish(t)
+        for t in range(tiles):
+            finish(t)
     else:
-        for residue in (2, 6, 1, 5, 3, 7):
-            make_phases(residue)
         repeat(tiles, turn_tile)
         for k in range(4):
 

time: 23.8 us -> 23.3 us (0.979)
  Pallas kernels: 9.66 us -> 9.16 us
    pallas_call x1, Pallas kernels: 5.32 us -> 4.82 us  [dedisperse(): pl.pallas_call(functools.partial(dedisperse_kernel, trials_each), in_spec...]
where the time goes in v6:
time: 23.3 us; the launch traced here: 23.1 us
  Pallas kernels  9.16 us (39%)
  starting transfers between devices  7.75 us (33%)
  waiting for transfers between devices  6.01 us (26%)
    ppermute x5, starting transfers between devices, swap(): return lax.ppermute(cells, ('bin', 'chan'), pairs)  7.75 us
    ppermute x5, waiting for transfers between devices, swap(): return lax.ppermute(cells, ('bin', 'chan'), pairs)  6.01 us
    pallas_call x1, Pallas kernels, dedisperse(): pl.pallas_call(functools.partial(dedisperse_kernel, trials_each), in_spec...  4.82 us
    pallas_call x1, Pallas kernels, search(): pl.pallas_call(functools.partial(search_kernel, scale), in_specs=[in_vmem...  3.03 us
    pallas_call x1, Pallas kernels, pick_templates(): pl.pallas_call(pick_kernel, out_shape=pltpu.VMEM((2 * count, 2 * taps), B...  1.31 us
  transfers between devices with their start and end apart: 5, of which 5 were waited for; matrix products, arithmetic and copies ran while one was open for 0% of the time, Pallas kernels for 6%

profile of v6, /device:TPU:0, one launch (start us, length us, event | category | flops | bytes accessed | tf_op | source)
XLA Modules:
  0.0 23.1 jit_solution(7411300349893790019)
XLA Ops:
  0.0 4.8 %dedisperse.1 = (bf16[64,1280]{1,0:T(8,128)(2,1)S(1)}, bf16[64,1280]{1,0:T(8,128)(2,1)S(1)}) custom-call(s32[1,64]{1,0:T(1,128)} %bitcast.10, s32[32,128]{1,0:T(8,128)} %bitcast.9, bf16[2,256,1024]{2,1,0:T(8,128)(2,1)} %sp_hbm.1), custom_call_target="tpu_custom_call" | custom-call | tf_op jit(solution)/shard_map/dedisperse/pallas_call | solution.py:273
  4.8 0.5 %collective-permute-start = (bf16[64,1280]{1,0:T(8,128)(2,1)S(1)}, bf16[64,1280]{1,0:T(8,128)(2,1)S(1)}, u32[]{:S(2)}, u32[]{:S(2)}) collective-permute-start(bf16[64,1280]{1,0:T(8,128)(2,1)S(1)} %get-tuple-element.11), channel_id=1, source_target_pairs={{0,1},{1,0},{2,3},{3,2},{4,5},{5,4},{6,7},{7,6},{8,9},{9,8},{10,11... | collective-permute-start | bytes 491528 | tf_op jit(solution)/shard_map/ppermute | solution.py:389
  5.3 1.0 %collective-permute-done = bf16[64,1280]{1,0:T(8,128)(2,1)S(1)} collective-permute-done((bf16[64,1280]{1,0:T(8,128)(2,1)S(1)}, bf16[64,1280]{1,0:T(8,128)(2,1)S(1)}, u32[]{:S(2)}, u32[]{:S(2)}) %collective-permute-start) | collective-permute-done | bytes 163872 | tf_op jit(solution)/shard_map/ppermute | solution.py:389
  6.5 3.9 %collective-permute-start.1 = (bf16[32,1024]{1,0:T(8,128)(2,1)S(1)}, bf16[32,1024]{1,0:T(8,128)(2,1)S(1)}, u32[]{:S(2)}, u32[]{:S(2)}) collective-permute-start(bf16[32,1024]{1,0:T(8,128)(2,1)S(1)} %get-tuple-element.12), channel_id=1, source_target_pairs={{0,6},{1,7},{2,4},{3,5},{4,2},{5,3},{6,0},{7,1},{8,14},{9,15},{10,... | collective-permute-start | bytes 196616 | tf_op jit(solution)/shard_map/ppermute | solution.py:389
  10.4 0.4 %collective-permute-start.2 = (bf16[32,1024]{1,0:T(8,128)(2,1)S(1)}, bf16[32,1024]{1,0:T(8,128)(2,1)S(1)}, u32[]{:S(2)}, u32[]{:S(2)}) collective-permute-start(bf16[32,1024]{1,0:T(8,128)(2,1)S(1)} %get-tuple-element.13), channel_id=1, source_target_pairs={{0,4},{1,5},{2,6},{3,7},{4,0},{5,1},{6,2},{7,3},{8,12},{9,13},{10,... | collective-permute-start | bytes 196616 | tf_op jit(solution)/shard_map/ppermute | solution.py:389
  10.8 0.2 collective-permute-start.3
  11.0 1.8 %collective-permute-done.1 = bf16[32,1024]{1,0:T(8,128)(2,1)S(1)} collective-permute-done((bf16[32,1024]{1,0:T(8,128)(2,1)S(1)}, bf16[32,1024]{1,0:T(8,128)(2,1)S(1)}, u32[]{:S(2)}, u32[]{:S(2)}) %collective-permute-start.1) | collective-permute-done | bytes 65568 | tf_op jit(solution)/shard_map/ppermute | solution.py:389
  12.8 1.9 %collective-permute-done.2 = bf16[32,1024]{1,0:T(8,128)(2,1)S(1)} collective-permute-done((bf16[32,1024]{1,0:T(8,128)(2,1)S(1)}, bf16[32,1024]{1,0:T(8,128)(2,1)S(1)}, u32[]{:S(2)}, u32[]{:S(2)}) %collective-permute-start.2) | collective-permute-done | bytes 65568 | tf_op jit(solution)/shard_map/ppermute | solution.py:389
  14.7 0.4 %collective-permute-done.3 = bf16[32,1024]{1,0:T(8,128)(2,1)S(1)} collective-permute-done((bf16[32,1024]{1,0:T(8,128)(2,1)S(1)}, bf16[32,1024]{1,0:T(8,128)(2,1)S(1)}, u32[]{:S(2)}, u32[]{:S(2)}) %collective-permute-start.3) | collective-permute-done | bytes 65568 | tf_op jit(solution)/shard_map/ppermute | solution.py:389
  15.2 2.7 %collective-permute-start.4 = (bf16[32,512]{1,0:T(8,128)(2,1)S(1)}, bf16[32,512]{1,0:T(8,128)(2,1)S(1)}, u32[]{:S(2)}, u32[]{:S(2)}) collective-permute-start(bf16[32,512]{1,0:T(8,128)(2,1)S(1)} %get-tuple-element.19), channel_id=1, source_target_pairs={{0,8},{1,9},{2,10},{3,11},{4,12},{5,13},{6,14},{7,15},{8,0},{9,1},... | collective-permute-start | bytes 98312 | tf_op jit(solution)/shard_map/ppermute | solution.py:389
  17.8 1.3 %pick_templates.1.templates_ref = bf16[256,512]{1,0:T(8,128)(2,1)S(1)} custom-call(bf16[2,256,256]{2,1,0:T(8,128)(2,1)} %bank_ref.1, s32[1,128]{1,0:T(1,128)} %bitcast.11), custom_call_target="tpu_custom_call" | custom-call | flops 33554432 | bytes 1048576 | tf_op jit(solution)/shard_map/pick_templates/pallas_call | solution.py:316
  19.1 0.9 %collective-permute-done.4.far_ref = bf16[32,512]{1,0:T(8,128)(2,1)S(1)} collective-permute-done((bf16[32,512]{1,0:T(8,128)(2,1)S(1)}, bf16[32,512]{1,0:T(8,128)(2,1)S(1)}, u32[]{:S(2)}, u32[]{:S(2)}) %collective-permute-start.4) | collective-permute-done | bytes 32800 | tf_op jit(solution)/shard_map/ppermute | solution.py:389
  20.1 3.0 %search.1 = bf16[16,128,256]{2,1,0:T(8,128)(2,1)} custom-call(bf16[32,512]{1,0:T(8,128)(2,1)S(1)} %get-tuple-element.20.near_ref, bf16[32,512]{1,0:T(8,128)(2,1)S(1)} %collective-permute-done.4.far_ref, bf16[256,512]{1,0:T(8,128)(2,1)S(1)} %pick_templates.1.templates_ref), custom_call_target="tpu_custom_call" | custom-call | tf_op jit(solution)/shard_map/search/pallas_call | solution.py:371
  (5 shorter events, 0.1 us)
Async XLA Ops:
  4.8 1.5 %collective-permute-start = (bf16[64,1280]{1,0:T(8,128)(2,1)S(1)}, bf16[64,1280]{1,0:T(8,128)(2,1)S(1)}, u32[]{:S(2)}, u32[]{:S(2)}) collective-permute-start(bf16[64,1280]{1,0:T(8,128)(2,1)S(1)} %get-tuple-element.11), channel_id=1, source_target_pairs={{0,1},{1,0},{2,3},{3,2},{4,5},{5,4},{6,7},{7,6},{8,9},{9,8},{10,11... | collective-permute-start | bytes 491528 | tf_op jit(solution)/shard_map/ppermute | solution.py:389
  6.5 6.3 %collective-permute-start.1 = (bf16[32,1024]{1,0:T(8,128)(2,1)S(1)}, bf16[32,1024]{1,0:T(8,128)(2,1)S(1)}, u32[]{:S(2)}, u32[]{:S(2)}) collective-permute-start(bf16[32,1024]{1,0:T(8,128)(2,1)S(1)} %get-tuple-element.12), channel_id=1, source_target_pairs={{0,6},{1,7},{2,4},{3,5},{4,2},{5,3},{6,0},{7,1},{8,14},{9,15},{10,... | collective-permute-start | bytes 196616 | tf_op jit(solution)/shard_map/ppermute | solution.py:389
  10.4 4.3 %collective-permute-start.2 = (bf16[32,1024]{1,0:T(8,128)(2,1)S(1)}, bf16[32,1024]{1,0:T(8,128)(2,1)S(1)}, u32[]{:S(2)}, u32[]{:S(2)}) collective-permute-start(bf16[32,1024]{1,0:T(8,128)(2,1)S(1)} %get-tuple-element.13), channel_id=1, source_target_pairs={{0,4},{1,5},{2,6},{3,7},{4,0},{5,1},{6,2},{7,3},{8,12},{9,13},{10,... | collective-permute-start | bytes 196616 | tf_op jit(solution)/shard_map/ppermute | solution.py:389
  10.8 4.3 %collective-permute-start.3 = (bf16[32,1024]{1,0:T(8,128)(2,1)S(1)}, bf16[32,1024]{1,0:T(8,128)(2,1)S(1)}, u32[]{:S(2)}, u32[]{:S(2)}) collective-permute-start(bf16[32,1024]{1,0:T(8,128)(2,1)S(1)} %get-tuple-element.14), channel_id=1, source_target_pairs={{0,2},{1,3},{2,0},{3,1},{4,6},{5,7},{6,4},{7,5},{8,10},{9,11},{10,... | collective-permute-start | bytes 196616 | tf_op jit(solution)/shard_map/ppermute | solution.py:389
  15.2 4.9 %collective-permute-start.4 = (bf16[32,512]{1,0:T(8,128)(2,1)S(1)}, bf16[32,512]{1,0:T(8,128)(2,1)S(1)}, u32[]{:S(2)}, u32[]{:S(2)}) collective-permute-start(bf16[32,512]{1,0:T(8,128)(2,1)S(1)} %get-tuple-element.19), channel_id=1, source_target_pairs={{0,8},{1,9},{2,10},{3,11},{4,12},{5,13},{6,14},{7,15},{8,0},{9,1},... | collective-permute-start | bytes 98312 | tf_op jit(solution)/shard_map/ppermute | solution.py:389

commit v7 on v6

--- a/solution.py
+++ b/solution.py
@@ -419,6 +419,7 @@
     send, send_far = by_parity(send)
     send_far, keep_far, send = lax.optimization_barrier((send_far, keep_far, send))
     keep = add(keep, swap(send_far, distance, 1), swap(keep_far, 0, 1), swap(send, distance, 0))
+    keep, templates = lax.optimization_barrier((keep, templates))
     part = spans // 2
     while True:
         width = (part // 2 - 1) * 2 * own_bins + own_bins + 2 * EDGE

time: 23.3 us -> 23.3 us (level)
  no operation moved by 1% of the time
where the time goes in v7:
time: 23.3 us; the launch traced here: 23.1 us
  Pallas kernels  9.15 us (39%)
  starting transfers between devices  7.75 us (33%)
  waiting for transfers between devices  6.01 us (26%)
    ppermute x5, starting transfers between devices, swap(): return lax.ppermute(cells, ('bin', 'chan'), pairs)  7.75 us
    ppermute x5, waiting for transfers between devices, swap(): return lax.ppermute(cells, ('bin', 'chan'), pairs)  6.01 us
    pallas_call x1, Pallas kernels, dedisperse(): pl.pallas_call(functools.partial(dedisperse_kernel, trials_each), in_spec...  4.82 us
    pallas_call x1, Pallas kernels, search(): pl.pallas_call(functools.partial(search_kernel, scale), in_specs=[in_vmem...  3.03 us
    pallas_call x1, Pallas kernels, pick_templates(): pl.pallas_call(pick_kernel, out_shape=pltpu.VMEM((2 * count, 2 * taps), B...  1.31 us
  transfers between devices with their start and end apart: 5, of which 5 were waited for; matrix products, arithmetic and copies ran while one was open for 0% of the time, Pallas kernels for 6%

profile of v7, /device:TPU:0, one launch (start us, length us, event | category | flops | bytes accessed | tf_op | source)
XLA Modules:
  0.0 23.1 jit_solution(15361179178369977586)
XLA Ops:
  0.0 4.8 %dedisperse.1 = (bf16[64,1280]{1,0:T(8,128)(2,1)S(1)}, bf16[64,1280]{1,0:T(8,128)(2,1)S(1)}) custom-call(s32[1,64]{1,0:T(1,128)} %bitcast.10, s32[32,128]{1,0:T(8,128)} %bitcast.9, bf16[2,256,1024]{2,1,0:T(8,128)(2,1)} %sp_hbm.1), custom_call_target="tpu_custom_call" | custom-call | tf_op jit(solution)/shard_map/dedisperse/pallas_call | solution.py:273
  4.8 0.5 %collective-permute-start = (bf16[64,1280]{1,0:T(8,128)(2,1)S(1)}, bf16[64,1280]{1,0:T(8,128)(2,1)S(1)}, u32[]{:S(2)}, u32[]{:S(2)}) collective-permute-start(bf16[64,1280]{1,0:T(8,128)(2,1)S(1)} %get-tuple-element.13), channel_id=1, source_target_pairs={{0,1},{1,0},{2,3},{3,2},{4,5},{5,4},{6,7},{7,6},{8,9},{9,8},{10,11... | collective-permute-start | bytes 491528 | tf_op jit(solution)/shard_map/ppermute | solution.py:389
  5.3 1.0 %collective-permute-done = bf16[64,1280]{1,0:T(8,128)(2,1)S(1)} collective-permute-done((bf16[64,1280]{1,0:T(8,128)(2,1)S(1)}, bf16[64,1280]{1,0:T(8,128)(2,1)S(1)}, u32[]{:S(2)}, u32[]{:S(2)}) %collective-permute-start) | collective-permute-done | bytes 163872 | tf_op jit(solution)/shard_map/ppermute | solution.py:389
  6.5 3.9 %collective-permute-start.1 = (bf16[32,1024]{1,0:T(8,128)(2,1)S(1)}, bf16[32,1024]{1,0:T(8,128)(2,1)S(1)}, u32[]{:S(2)}, u32[]{:S(2)}) collective-permute-start(bf16[32,1024]{1,0:T(8,128)(2,1)S(1)} %get-tuple-element.14), channel_id=1, source_target_pairs={{0,6},{1,7},{2,4},{3,5},{4,2},{5,3},{6,0},{7,1},{8,14},{9,15},{10,... | collective-permute-start | bytes 196616 | tf_op jit(solution)/shard_map/ppermute | solution.py:389
  10.4 0.4 %collective-permute-start.2 = (bf16[32,1024]{1,0:T(8,128)(2,1)S(1)}, bf16[32,1024]{1,0:T(8,128)(2,1)S(1)}, u32[]{:S(2)}, u32[]{:S(2)}) collective-permute-start(bf16[32,1024]{1,0:T(8,128)(2,1)S(1)} %get-tuple-element.15), channel_id=1, source_target_pairs={{0,4},{1,5},{2,6},{3,7},{4,0},{5,1},{6,2},{7,3},{8,12},{9,13},{10,... | collective-permute-start | bytes 196616 | tf_op jit(solution)/shard_map/ppermute | solution.py:389
  10.8 0.2 collective-permute-start.3
  11.0 1.3 %pick_templates.1.templates_ref = bf16[256,512]{1,0:T(8,128)(2,1)S(1)} custom-call(bf16[2,256,256]{2,1,0:T(8,128)(2,1)} %bank_ref.1, s32[1,128]{1,0:T(1,128)} %bitcast.11), custom_call_target="tpu_custom_call" | custom-call | flops 33554432 | bytes 1048576 | tf_op jit(solution)/shard_map/pick_templates/pallas_call | solution.py:316
  12.4 0.4 %collective-permute-done.1 = bf16[32,1024]{1,0:T(8,128)(2,1)S(1)} collective-permute-done((bf16[32,1024]{1,0:T(8,128)(2,1)S(1)}, bf16[32,1024]{1,0:T(8,128)(2,1)S(1)}, u32[]{:S(2)}, u32[]{:S(2)}) %collective-permute-start.1) | collective-permute-done | bytes 65568 | tf_op jit(solution)/shard_map/ppermute | solution.py:389
  12.8 1.9 %collective-permute-done.2 = bf16[32,1024]{1,0:T(8,128)(2,1)S(1)} collective-permute-done((bf16[32,1024]{1,0:T(8,128)(2,1)S(1)}, bf16[32,1024]{1,0:T(8,128)(2,1)S(1)}, u32[]{:S(2)}, u32[]{:S(2)}) %collective-permute-start.2) | collective-permute-done | bytes 65568 | tf_op jit(solution)/shard_map/ppermute | solution.py:389
  14.7 0.4 %collective-permute-done.3 = bf16[32,1024]{1,0:T(8,128)(2,1)S(1)} collective-permute-done((bf16[32,1024]{1,0:T(8,128)(2,1)S(1)}, bf16[32,1024]{1,0:T(8,128)(2,1)S(1)}, u32[]{:S(2)}, u32[]{:S(2)}) %collective-permute-start.3) | collective-permute-done | bytes 65568 | tf_op jit(solution)/shard_map/ppermute | solution.py:389
  15.2 2.7 %collective-permute-start.4 = (bf16[32,512]{1,0:T(8,128)(2,1)S(1)}, bf16[32,512]{1,0:T(8,128)(2,1)S(1)}, u32[]{:S(2)}, u32[]{:S(2)}) collective-permute-start(bf16[32,512]{1,0:T(8,128)(2,1)S(1)} %get-tuple-element.23), channel_id=1, source_target_pairs={{0,8},{1,9},{2,10},{3,11},{4,12},{5,13},{6,14},{7,15},{8,0},{9,1},... | collective-permute-start | bytes 98312 | tf_op jit(solution)/shard_map/ppermute | solution.py:389
  17.8 2.2 %collective-permute-done.4.far_ref = bf16[32,512]{1,0:T(8,128)(2,1)S(1)} collective-permute-done((bf16[32,512]{1,0:T(8,128)(2,1)S(1)}, bf16[32,512]{1,0:T(8,128)(2,1)S(1)}, u32[]{:S(2)}, u32[]{:S(2)}) %collective-permute-start.4) | collective-permute-done | bytes 32800 | tf_op jit(solution)/shard_map/ppermute | solution.py:389
  20.1 3.0 %search.1 = bf16[16,128,256]{2,1,0:T(8,128)(2,1)} custom-call(bf16[32,512]{1,0:T(8,128)(2,1)S(1)} %get-tuple-element.24.near_ref, bf16[32,512]{1,0:T(8,128)(2,1)S(1)} %collective-permute-done.4.far_ref, bf16[256,512]{1,0:T(8,128)(2,1)S(1)} %pick_templates.1.templates_ref), custom_call_target="tpu_custom_call" | custom-call | tf_op jit(solution)/shard_map/search/pallas_call | solution.py:371
  (5 shorter events, 0.1 us)
Async XLA Ops:
  4.8 1.5 %collective-permute-start = (bf16[64,1280]{1,0:T(8,128)(2,1)S(1)}, bf16[64,1280]{1,0:T(8,128)(2,1)S(1)}, u32[]{:S(2)}, u32[]{:S(2)}) collective-permute-start(bf16[64,1280]{1,0:T(8,128)(2,1)S(1)} %get-tuple-element.13), channel_id=1, source_target_pairs={{0,1},{1,0},{2,3},{3,2},{4,5},{5,4},{6,7},{7,6},{8,9},{9,8},{10,11... | collective-permute-start | bytes 491528 | tf_op jit(solution)/shard_map/ppermute | solution.py:389
  6.5 6.3 %collective-permute-start.1 = (bf16[32,1024]{1,0:T(8,128)(2,1)S(1)}, bf16[32,1024]{1,0:T(8,128)(2,1)S(1)}, u32[]{:S(2)}, u32[]{:S(2)}) collective-permute-start(bf16[32,1024]{1,0:T(8,128)(2,1)S(1)} %get-tuple-element.14), channel_id=1, source_target_pairs={{0,6},{1,7},{2,4},{3,5},{4,2},{5,3},{6,0},{7,1},{8,14},{9,15},{10,... | collective-permute-start | bytes 196616 | tf_op jit(solution)/shard_map/ppermute | solution.py:389
  10.4 4.3 %collective-permute-start.2 = (bf16[32,1024]{1,0:T(8,128)(2,1)S(1)}, bf16[32,1024]{1,0:T(8,128)(2,1)S(1)}, u32[]{:S(2)}, u32[]{:S(2)}) collective-permute-start(bf16[32,1024]{1,0:T(8,128)(2,1)S(1)} %get-tuple-element.15), channel_id=1, source_target_pairs={{0,4},{1,5},{2,6},{3,7},{4,0},{5,1},{6,2},{7,3},{8,12},{9,13},{10,... | collective-permute-start | bytes 196616 | tf_op jit(solution)/shard_map/ppermute | solution.py:389
  10.8 4.3 %collective-permute-start.3 = (bf16[32,1024]{1,0:T(8,128)(2,1)S(1)}, bf16[32,1024]{1,0:T(8,128)(2,1)S(1)}, u32[]{:S(2)}, u32[]{:S(2)}) collective-permute-start(bf16[32,1024]{1,0:T(8,128)(2,1)S(1)} %get-tuple-element.16), channel_id=1, source_target_pairs={{0,2},{1,3},{2,0},{3,1},{4,6},{5,7},{6,4},{7,5},{8,10},{9,11},{10,... | collective-permute-start | bytes 196616 | tf_op jit(solution)/shard_map/ppermute | solution.py:389
  15.2 4.9 %collective-permute-start.4 = (bf16[32,512]{1,0:T(8,128)(2,1)S(1)}, bf16[32,512]{1,0:T(8,128)(2,1)S(1)}, u32[]{:S(2)}, u32[]{:S(2)}) collective-permute-start(bf16[32,512]{1,0:T(8,128)(2,1)S(1)} %get-tuple-element.23), channel_id=1, source_target_pairs={{0,8},{1,9},{2,10},{3,11},{4,12},{5,13},{6,14},{7,15},{8,0},{9,1},... | collective-permute-start | bytes 98312 | tf_op jit(solution)/shard_map/ppermute | solution.py:389

commit v8 on v6

--- a/solution.py
+++ b/solution.py
@@ -238,7 +238,7 @@
     sizes = [min(size, bins // s) for s in STEP]
     counts = [bins // s // own for s, own in zip(STEP, sizes)]
     if tiles <= 8:
-        work = [(k, b, sizes[k]) for k in (0, 1, 2, 3) for b in range(counts[k])]
+        work = [(k, b, sizes[k]) for k in (1, 0, 2, 3) for b in range(counts[k])]
         buffers = (y0, y1)
         for t in range(tiles):
             turn_tile(t)

time: 23.3 us -> 23.3 us (level)
  no operation moved by 1% of the time
where the time goes in v8:
time: 23.3 us; the launch traced here: 23.1 us
  Pallas kernels  9.13 us (39%)
  starting transfers between devices  7.74 us (33%)
  waiting for transfers between devices  6.02 us (26%)
    ppermute x5, starting transfers between devices, swap(): return lax.ppermute(cells, ('bin', 'chan'), pairs)  7.74 us
    ppermute x5, waiting for transfers between devices, swap(): return lax.ppermute(cells, ('bin', 'chan'), pairs)  6.02 us
    pallas_call x1, Pallas kernels, dedisperse(): pl.pallas_call(functools.partial(dedisperse_kernel, trials_each), in_spec...  4.78 us
    pallas_call x1, Pallas kernels, search(): pl.pallas_call(functools.partial(search_kernel, scale), in_specs=[in_vmem...  3.04 us
    pallas_call x1, Pallas kernels, pick_templates(): pl.pallas_call(pick_kernel, out_shape=pltpu.VMEM((2 * count, 2 * taps), B...  1.31 us
  transfers between devices with their start and end apart: 5, of which 5 were waited for; matrix products, arithmetic and copies ran while one was open for 0% of the time, Pallas kernels for 6%

profile of v8, /device:TPU:0, one launch (start us, length us, event | category | flops | bytes accessed | tf_op | source)
XLA Modules:
  0.0 23.1 jit_solution(97829733131372477)
XLA Ops:
  0.0 4.8 %dedisperse.1 = (bf16[64,1280]{1,0:T(8,128)(2,1)S(1)}, bf16[64,1280]{1,0:T(8,128)(2,1)S(1)}) custom-call(s32[1,64]{1,0:T(1,128)} %bitcast.10, s32[32,128]{1,0:T(8,128)} %bitcast.9, bf16[2,256,1024]{2,1,0:T(8,128)(2,1)} %sp_hbm.1), custom_call_target="tpu_custom_call" | custom-call | tf_op jit(solution)/shard_map/dedisperse/pallas_call | solution.py:273
  4.8 0.5 %collective-permute-start = (bf16[64,1280]{1,0:T(8,128)(2,1)S(1)}, bf16[64,1280]{1,0:T(8,128)(2,1)S(1)}, u32[]{:S(2)}, u32[]{:S(2)}) collective-permute-start(bf16[64,1280]{1,0:T(8,128)(2,1)S(1)} %get-tuple-element.11), channel_id=1, source_target_pairs={{0,1},{1,0},{2,3},{3,2},{4,5},{5,4},{6,7},{7,6},{8,9},{9,8},{10,11... | collective-permute-start | bytes 491528 | tf_op jit(solution)/shard_map/ppermute | solution.py:389
  5.3 1.0 %collective-permute-done = bf16[64,1280]{1,0:T(8,128)(2,1)S(1)} collective-permute-done((bf16[64,1280]{1,0:T(8,128)(2,1)S(1)}, bf16[64,1280]{1,0:T(8,128)(2,1)S(1)}, u32[]{:S(2)}, u32[]{:S(2)}) %collective-permute-start) | collective-permute-done | bytes 163872 | tf_op jit(solution)/shard_map/ppermute | solution.py:389
  6.4 3.9 %collective-permute-start.1 = (bf16[32,1024]{1,0:T(8,128)(2,1)S(1)}, bf16[32,1024]{1,0:T(8,128)(2,1)S(1)}, u32[]{:S(2)}, u32[]{:S(2)}) collective-permute-start(bf16[32,1024]{1,0:T(8,128)(2,1)S(1)} %get-tuple-element.12), channel_id=1, source_target_pairs={{0,6},{1,7},{2,4},{3,5},{4,2},{5,3},{6,0},{7,1},{8,14},{9,15},{10,... | collective-permute-start | bytes 196616 | tf_op jit(solution)/shard_map/ppermute | solution.py:389
  10.4 0.5 %collective-permute-start.2 = (bf16[32,1024]{1,0:T(8,128)(2,1)S(1)}, bf16[32,1024]{1,0:T(8,128)(2,1)S(1)}, u32[]{:S(2)}, u32[]{:S(2)}) collective-permute-start(bf16[32,1024]{1,0:T(8,128)(2,1)S(1)} %get-tuple-element.13), channel_id=1, source_target_pairs={{0,4},{1,5},{2,6},{3,7},{4,0},{5,1},{6,2},{7,3},{8,12},{9,13},{10,... | collective-permute-start | bytes 196616 | tf_op jit(solution)/shard_map/ppermute | solution.py:389
  10.8 0.2 collective-permute-start.3
  11.0 1.8 %collective-permute-done.1 = bf16[32,1024]{1,0:T(8,128)(2,1)S(1)} collective-permute-done((bf16[32,1024]{1,0:T(8,128)(2,1)S(1)}, bf16[32,1024]{1,0:T(8,128)(2,1)S(1)}, u32[]{:S(2)}, u32[]{:S(2)}) %collective-permute-start.1) | collective-permute-done | bytes 65568 | tf_op jit(solution)/shard_map/ppermute | solution.py:389
  12.8 1.9 %collective-permute-done.2 = bf16[32,1024]{1,0:T(8,128)(2,1)S(1)} collective-permute-done((bf16[32,1024]{1,0:T(8,128)(2,1)S(1)}, bf16[32,1024]{1,0:T(8,128)(2,1)S(1)}, u32[]{:S(2)}, u32[]{:S(2)}) %collective-permute-start.2) | collective-permute-done | bytes 65568 | tf_op jit(solution)/shard_map/ppermute | solution.py:389
  14.6 0.5 %collective-permute-done.3 = bf16[32,1024]{1,0:T(8,128)(2,1)S(1)} collective-permute-done((bf16[32,1024]{1,0:T(8,128)(2,1)S(1)}, bf16[32,1024]{1,0:T(8,128)(2,1)S(1)}, u32[]{:S(2)}, u32[]{:S(2)}) %collective-permute-start.3) | collective-permute-done | bytes 65568 | tf_op jit(solution)/shard_map/ppermute | solution.py:389
  15.1 2.7 %collective-permute-start.4 = (bf16[32,512]{1,0:T(8,128)(2,1)S(1)}, bf16[32,512]{1,0:T(8,128)(2,1)S(1)}, u32[]{:S(2)}, u32[]{:S(2)}) collective-permute-start(bf16[32,512]{1,0:T(8,128)(2,1)S(1)} %get-tuple-element.19), channel_id=1, source_target_pairs={{0,8},{1,9},{2,10},{3,11},{4,12},{5,13},{6,14},{7,15},{8,0},{9,1},... | collective-permute-start | bytes 98312 | tf_op jit(solution)/shard_map/ppermute | solution.py:389
  17.8 1.3 %pick_templates.1.templates_ref = bf16[256,512]{1,0:T(8,128)(2,1)S(1)} custom-call(bf16[2,256,256]{2,1,0:T(8,128)(2,1)} %bank_ref.1, s32[1,128]{1,0:T(1,128)} %bitcast.11), custom_call_target="tpu_custom_call" | custom-call | flops 33554432 | bytes 1048576 | tf_op jit(solution)/shard_map/pick_templates/pallas_call | solution.py:316
  19.1 0.9 %collective-permute-done.4.far_ref = bf16[32,512]{1,0:T(8,128)(2,1)S(1)} collective-permute-done((bf16[32,512]{1,0:T(8,128)(2,1)S(1)}, bf16[32,512]{1,0:T(8,128)(2,1)S(1)}, u32[]{:S(2)}, u32[]{:S(2)}) %collective-permute-start.4) | collective-permute-done | bytes 32800 | tf_op jit(solution)/shard_map/ppermute | solution.py:389
  20.0 3.0 %search.1 = bf16[16,128,256]{2,1,0:T(8,128)(2,1)} custom-call(bf16[32,512]{1,0:T(8,128)(2,1)S(1)} %get-tuple-element.20.near_ref, bf16[32,512]{1,0:T(8,128)(2,1)S(1)} %collective-permute-done.4.far_ref, bf16[256,512]{1,0:T(8,128)(2,1)S(1)} %pick_templates.1.templates_ref), custom_call_target="tpu_custom_call" | custom-call | tf_op jit(solution)/shard_map/search/pallas_call | solution.py:371
  (5 shorter events, 0.1 us)
Async XLA Ops:
  4.8 1.5 %collective-permute-start = (bf16[64,1280]{1,0:T(8,128)(2,1)S(1)}, bf16[64,1280]{1,0:T(8,128)(2,1)S(1)}, u32[]{:S(2)}, u32[]{:S(2)}) collective-permute-start(bf16[64,1280]{1,0:T(8,128)(2,1)S(1)} %get-tuple-element.11), channel_id=1, source_target_pairs={{0,1},{1,0},{2,3},{3,2},{4,5},{5,4},{6,7},{7,6},{8,9},{9,8},{10,11... | collective-permute-start | bytes 491528 | tf_op jit(solution)/shard_map/ppermute | solution.py:389
  6.4 6.3 %collective-permute-start.1 = (bf16[32,1024]{1,0:T(8,128)(2,1)S(1)}, bf16[32,1024]{1,0:T(8,128)(2,1)S(1)}, u32[]{:S(2)}, u32[]{:S(2)}) collective-permute-start(bf16[32,1024]{1,0:T(8,128)(2,1)S(1)} %get-tuple-element.12), channel_id=1, source_target_pairs={{0,6},{1,7},{2,4},{3,5},{4,2},{5,3},{6,0},{7,1},{8,14},{9,15},{10,... | collective-permute-start | bytes 196616 | tf_op jit(solution)/shard_map/ppermute | solution.py:389
  10.4 4.3 %collective-permute-start.2 = (bf16[32,1024]{1,0:T(8,128)(2,1)S(1)}, bf16[32,1024]{1,0:T(8,128)(2,1)S(1)}, u32[]{:S(2)}, u32[]{:S(2)}) collective-permute-start(bf16[32,1024]{1,0:T(8,128)(2,1)S(1)} %get-tuple-element.13), channel_id=1, source_target_pairs={{0,4},{1,5},{2,6},{3,7},{4,0},{5,1},{6,2},{7,3},{8,12},{9,13},{10,... | collective-permute-start | bytes 196616 | tf_op jit(solution)/shard_map/ppermute | solution.py:389
  10.8 4.3 %collective-permute-start.3 = (bf16[32,1024]{1,0:T(8,128)(2,1)S(1)}, bf16[32,1024]{1,0:T(8,128)(2,1)S(1)}, u32[]{:S(2)}, u32[]{:S(2)}) collective-permute-start(bf16[32,1024]{1,0:T(8,128)(2,1)S(1)} %get-tuple-element.14), channel_id=1, source_target_pairs={{0,2},{1,3},{2,0},{3,1},{4,6},{5,7},{6,4},{7,5},{8,10},{9,11},{10,... | collective-permute-start | bytes 196616 | tf_op jit(solution)/shard_map/ppermute | solution.py:389
  15.1 4.9 %collective-permute-start.4 = (bf16[32,512]{1,0:T(8,128)(2,1)S(1)}, bf16[32,512]{1,0:T(8,128)(2,1)S(1)}, u32[]{:S(2)}, u32[]{:S(2)}) collective-permute-start(bf16[32,512]{1,0:T(8,128)(2,1)S(1)} %get-tuple-element.19), channel_id=1, source_target_pairs={{0,8},{1,9},{2,10},{3,11},{4,12},{5,13},{6,14},{7,15},{8,0},{9,1},... | collective-permute-start | bytes 98312 | tf_op jit(solution)/shard_map/ppermute | solution.py:389
